TPU v7x, 256 devices: a whole 4x4x8 slice. The times are simulated.
256 devices in a mesh: dp: 8 (over z), expert: 32 (over y, x, core).
Axes of the slice: x: 4, y: 4, z: 8, core: 2. Of those that a mesh axis runs over, the one named last changes fastest.
Arguments:
- hidden_in: bfloat16 [32768, 1024], P(('dp', 'expert')), may hold values from -6 to 6
- rank_grad: bfloat16 [32768, 1024], P(('dp', 'expert')), may hold values from -6 to 6
- gates: bfloat16 [32768, 8], P(('dp', 'expert')), may hold values from 0.049804688 to 1
- expert_ids: int32 [32768, 8], P(('dp', 'expert')), may hold values from 0 to 63, all different within a row; in each aligned block of 128 rows (0 to 127, 128 to 255, ...) at most 32 rows name the same one
- cores: bfloat16 [64, 1024, 1024], P('expert'), may hold values from -0.1875 to 0.1875
Outputs:
- rank_input_grad: bfloat16 [32768, 1024], P(('dp', 'expert'))
- core_grad: float32 [1024, 64, 1024], P('dp', 'expert')
Inputs may be any that keep to these rules, and one draw needn't show every extreme that they name: `expert_ids`: each row names 8 different experts; among the rows of one device no expert is named more than 32 times, a bound that some block reaches.
All inputs are finite; a program needn't handle non-finite values.
Results may differ from a plain program's by a relative error of at most 0.0057.
Values may be sent and summed in bfloat16 or wider, within the bound.
A program may use at most 128 MiB of HBM per device.

v0:
```python
import jax
import jax.numpy as jnp
from jax import lax
from jax.sharding import PartitionSpec as P


def slot_table(chosen, experts, capacity):
    labels = jnp.arange(experts, dtype=jnp.int32)
    onehot = (chosen[..., None] == labels).astype(jnp.int32)
    before = jnp.cumsum(onehot, axis=-2) - onehot
    places = jnp.sum(before * onehot, axis=-1)
    return chosen * capacity + places


def expert_work(sent_z, sent_r, sent_g, cores):
    upper = jnp.einsum("slcr,lrq->slcq", sent_z, cores, preferred_element_type=jnp.float32)
    sig = jax.nn.sigmoid(upper)
    slope = sig * (1.0 + upper * (1.0 - sig))
    lowered = (sent_r.astype(jnp.float32) * sent_g.astype(jnp.float32)[..., None] * slope).astype(
        jnp.bfloat16
    )
    back = jnp.einsum("slcq,lrq->slcr", lowered, cores, preferred_element_type=jnp.float32).astype(
        jnp.bfloat16
    )
    return (lowered, back)


def local(hidden_in, rank_grad, gates, expert_ids, cores):
    tok_dev, rank = hidden_in.shape
    topk = gates.shape[1]
    exp_dev = cores.shape[0]
    groups = lax.axis_size("expert")
    experts = exp_dev * groups
    capacity = 2 * tok_dev * topk // experts
    width = exp_dev * capacity
    pairs = tok_dev * topk
    zero_half = jnp.zeros((), jnp.bfloat16)
    own_slots = slot_table(expert_ids.reshape(pairs), experts, capacity)
    owners = (
        jnp.full((experts * capacity,), -1, jnp.int32)
        .at[own_slots]
        .set(jnp.arange(pairs, dtype=jnp.int32))
    )
    filled = owners >= 0
    picks = jnp.maximum(owners, 0)
    send_z = jnp.where(filled[:, None], hidden_in[picks // topk], zero_half).reshape(
        groups, width, rank
    )
    send_r = jnp.where(filled[:, None], rank_grad[picks // topk], zero_half).reshape(
        groups, width, rank
    )
    send_g = jnp.where(filled, gates.reshape(pairs)[picks], zero_half).reshape(groups, width)
    recv_z, recv_r, recv_g = (
        lax.all_to_all(send_z, "expert", split_axis=0, concat_axis=0, tiled=True),
        lax.all_to_all(send_r, "expert", split_axis=0, concat_axis=0, tiled=True),
        lax.all_to_all(send_g, "expert", split_axis=0, concat_axis=0, tiled=True),
    )
    recv_z = recv_z.reshape(groups, exp_dev, capacity, rank)
    recv_r = recv_r.reshape(groups, exp_dev, capacity, rank)
    recv_g = recv_g.reshape(groups, exp_dev, capacity)
    lowered, back = expert_work(recv_z, recv_r, recv_g, cores)
    returned = lax.all_to_all(
        back.reshape(groups, width, rank), "expert", split_axis=0, concat_axis=0, tiled=True
    )
    flat_back = returned.reshape(experts * capacity, rank)
    per_pair = flat_back[own_slots].astype(jnp.float32).reshape(tok_dev, topk, rank)
    rank_input_grad = jnp.sum(per_pair, axis=1).astype(jnp.bfloat16)
    term = jnp.einsum("slcj,slcq->jlq", recv_z, lowered, preferred_element_type=jnp.float32)
    core_grad = lax.psum_scatter(term, "dp", scatter_dimension=0, tiled=True)
    return (rank_input_grad, core_grad)


def solution(mesh):
    in_specs = (
        P(("dp", "expert"), None),
        P(("dp", "expert"), None),
        P(("dp", "expert"), None),
        P(("dp", "expert"), None),
        P("expert", None, None),
    )
    out_specs = (P(("dp", "expert"), None), P("dp", "expert", None))
    return jax.shard_map(local, mesh=mesh, in_specs=in_specs, out_specs=out_specs, check_vma=False)
```

profile of v0, /device:TPU:1, one launch (start us, length us, event | category | flops | bytes accessed | tf_op | source)
XLA Modules:
  0.0 319.0 jit_solution(16397553553456612683)
XLA Ops:
  7.2 0.0 copy-start
  7.2 0.8 copy.24
  8.0 0.1 eq.29
  8.1 0.1 eq.25
  8.2 0.7 broadcast_multiply_fusion
  8.9 18.0 %reduce-window.6 = s32[64,8,128]{2,1,0:T(8,128)S(1)} reduce-window(s32[64,8,128]{2,1,0:T(8,128)S(1)} %fusion.21, s32[]{:T(128)} %constant.34.clone.1), window={size=1x1x128 pad=0_0x0_0x127_0}, to_apply=%region_0.0 | reduce-window | flops 8323072 | bytes 524292 | tf_op jit(solution)/shard_map/reduce-window
  26.9 0.1 slice.16
  27.1 0.1 copy.26
  27.2 0.1 copy.27
  27.3 0.1 broadcast_add_fusion
  27.5 0.1 copy.23
  27.6 0.1 mul.38
  27.7 0.1 fusion.20
  27.8 4.3 %scatter_custom_fusion = s32[2048]{0:T(1024)S(1)} fusion(s32[1024]{0:T(1024)S(1)} %bitcast.74, s32[1024]{0:T(1024)S(1)} %iota.11, s32[]{:T(128)} %constant.32.clone.1), kind=kCustom, calls=%fused_computation.44 | custom fusion | bytes 8196 | tf_op jit(solution)/shard_map/scatter | solution.py:42
  32.1 0.8 copy.28
  32.9 0.1 reshape.95
  33.0 13.1 %gather_fusion.1 = bf16[2048]{0:T(1024)(128)(2,1)S(1)} fusion(bf16[1024]{0:T(1024)(128)(2,1)S(1)} %reshape.95, s32[2048]{0:T(1024)S(1)} %get-tuple-element.10), kind=kCustom, calls=%fused_computation.1 | custom fusion | bytes 16384 | tf_op jit(solution)/shard_map/gather | solution.py:52
  46.1 0.7 all_to_all.20
  46.8 8.6 %all-to-all-start.1 = ((bf16[32,1,64]{2,1,0:T(2,128)(2,1)}), bf16[32,1,64]{2,1,0:T(2,128)(2,1)S(1)}, u32[]{:S(2)}, u32[]{:S(2)}) async-start(bf16[32,1,64]{2,1,0:T(2,128)(2,1)} %all_to_all.20), calls=%async_computation.1 | async-start | bytes 32768 | tf_op jit(solution)/shard_map/all_to_all | solution.py:56
  55.4 0.1 broadcast_in_dim.39
  55.5 0.0 copy-done
  55.5 0.0 copy-start.1
  55.5 9.6 %gather_fusion = bf16[2048,1024]{1,0:T(8,128)(2,1)} fusion(bf16[128,1024]{1,0:T(8,128)(2,1)S(1)} %copy-done, s32[2048]{0:T(1024)S(1)} %get-tuple-element.11), kind=kCustom, calls=%fused_computation | custom fusion | bytes 8396800 | tf_op jit(solution)/shard_map/gather | solution.py:49
  65.1 0.0 copy-done.1
  65.1 9.7 %gather_fusion.2 = bf16[2048,1024]{1,0:T(8,128)(2,1)} fusion(bf16[128,1024]{1,0:T(8,128)(2,1)S(1)} %copy-done.1, s32[2048]{0:T(1024)S(1)} %get-tuple-element.11), kind=kCustom, calls=%fused_computation.2 | custom fusion | bytes 8396800 | tf_op jit(solution)/shard_map/gather | solution.py:46
  74.8 5.8 %broadcast_select_fusion = (bf16[32,64,1024]{2,1,0:T(8,128)(2,1)}, bf16[32,64,1024]{2,1,0:T(8,128)(2,1)}) fusion(bf16[32,64,1024]{2,1,0:T(8,128)(2,1)} %bitcast.67, pred[32,64]{1,0:T(8,128)(4,1)S(1)} %broadcast_in_dim.39, bf16[32,64,1024]{2,1,0:T(8,128)(2,1)} %bitcast.66), kind=kLoop, calls=%fused_computation.19 | loop fusion | flops 4194304 | bytes 16779264 | tf_op jit(solution)/shard_map/jit(_where)/select_n | solution.py:46
  80.6 0.0 all-to-all-done.1
  80.6 58.4 %all_to_all.25 = bf16[32,64,1024]{2,1,0:T(8,128)(2,1)} all-to-all(bf16[32,64,1024]{2,1,0:T(8,128)(2,1)} %get-tuple-element.12), channel_id=1, replica_groups=mesh['dp'=8,'expert'=32] {'expert'}, dimensions={0} | all-to-all | bytes 8388608 | tf_op jit(solution)/shard_map/all_to_all | solution.py:54
  139.0 4.8 %all-to-all-start = ((bf16[32,64,1024]{2,1,0:T(8,128)(2,1)}), bf16[32,64,1024]{2,1,0:T(8,128)(2,1)}, u32[]{:S(2)}, u32[]{:S(2)}) async-start(bf16[32,64,1024]{2,1,0:T(8,128)(2,1)} %get-tuple-element.13), calls=%async_computation | async-start | bytes 8388608 | tf_op jit(solution)/shard_map/all_to_all | solution.py:55
  143.8 0.2 reduce-scatter.2.cloned.1.call-start
  144.0 0.1 convert_reduce_fusion
  144.1 0.1 reshape.100
  144.2 50.0 %all-to-all-done = bf16[32,64,1024]{2,1,0:T(8,128)(2,1)} async-done(((bf16[32,64,1024]{2,1,0:T(8,128)(2,1)}), bf16[32,64,1024]{2,1,0:T(8,128)(2,1)}, u32[]{:S(2)}, u32[]{:S(2)}) %all-to-all-start) | async-done | bytes 4194336 | tf_op jit(solution)/shard_map/all_to_all | solution.py:55
  194.2 0.0 copy-start.2
  194.2 10.5 %fusion.6 = bf16[32,2,32,1024]{3,2,0,1:T(8,128)(2,1)S(1)} fusion(bf16[2,1024,1024]{2,1,0:T(8,128)(2,1)} %param.9, f32[32,2,32]{2,0,1:T(8,128)S(1)} %copy.30, bf16[32,2,32,1024]{3,2,1,0:T(8,128)(2,1)} %bitcast.69, bf16[32,2,32,1024]{3,2,1,0:T(8,128)(2,1)} %bitcast.18), kind=kOutput, calls=%fused_computation.13 | convolution fusion | flops 4318035968 | bytes 16785408 | tf_op jit(solution)/shard_map/slcr,lrq->slcq/dot_general | solution.py:16
  204.7 0.0 copy-start.3
  204.7 2.0 copy-done.3
  206.7 0.0 copy-done.2
  206.7 6.9 %fusion.13 = f32[1024,2,1024]{0,2,1:T(8,128)} fusion(bf16[32,2,32,1024]{3,2,0,1:T(8,128)(2,1)S(1)} %fusion.6, bf16[32,2,32,1024]{3,2,1,0:T(8,128)(2,1)S(1)} %bitcast.70), kind=kOutput, calls=%fused_computation.24 | convolution fusion | flops 4294967296 | bytes 16777216 | tf_op jit(solution)/shard_map/slcj,slcq->jlq/dot_general | solution.py:68
  213.5 0.0 reduce-scatter.2.cloned.1.call-update
  213.6 8.0 %convert_bitcast_fusion = bf16[32,2,32,1024]{3,2,0,1:T(8,128)(2,1)S(1)} fusion(bf16[32,2,32,1024]{3,2,0,1:T(8,128)(2,1)} %copy-done.3, bf16[2,1024,1024]{2,1,0:T(8,128)(2,1)} %param.9), kind=kOutput, calls=%fused_computation.18 | convolution fusion | flops 4297064448 | bytes 12582912 | tf_op jit(solution)/shard_map/slcq,lrq->slcr/dot_general | solution.py:22
  221.6 2.5 copy.33
  224.0 8.1 %all-to-all-start.3 = ((bf16[32,64,1024]{2,1,0:T(8,128)(2,1)}), bf16[32,64,1024]{2,1,0:T(8,128)(2,1)}, u32[]{:S(2)}, u32[]{:S(2)}) async-start(bf16[32,64,1024]{2,1,0:T(8,128)(2,1)} %bitcast.68), calls=%async_computation.3 | async-start | bytes 8388608 | tf_op jit(solution)/shard_map/all_to_all | solution.py:62
  232.1 50.2 %all-to-all-done.3 = bf16[32,64,1024]{2,1,0:T(8,128)(2,1)} async-done(((bf16[32,64,1024]{2,1,0:T(8,128)(2,1)}), bf16[32,64,1024]{2,1,0:T(8,128)(2,1)}, u32[]{:S(2)}, u32[]{:S(2)}) %all-to-all-start.3) | async-done | bytes 4194336 | tf_op jit(solution)/shard_map/all_to_all | solution.py:62
  282.4 7.7 %gather_fusion.3 = bf16[1024,1024]{1,0:T(8,128)(2,1)S(1)} fusion(bf16[2048,1024]{1,0:T(8,128)(2,1)} %bitcast.13, s32[1024]{0:T(1024)S(1)} %broadcast_clamp_fusion), kind=kCustom, calls=%fused_computation.3 | custom fusion | bytes 4198400 | tf_op jit(solution)/shard_map/gather | solution.py:66
  290.1 2.1 bitcast_reduce_fusion
  292.2 17.7 %reduce-scatter.2.cloned.1.call-done = f32[128,2,1024]{0,2,1:T(8,128)} async-done(((f32[1024,2,1024]{0,2,1:T(8,128)}), f32[128,2,1024]{0,2,1:T(8,128)}) %reduce-scatter.2.cloned.1.call-update) | async-done | bytes 1048592 | tf_op jit(solution)/shard_map/reduce_scatter | solution.py:69
  309.9 2.3 copy.35
  (9 shorter events, 0.1 us)
Async XLA Ops:
  7.2 48.3 %copy-start = (bf16[128,1024]{1,0:T(8,128)(2,1)S(1)}, bf16[128,1024]{1,0:T(8,128)(2,1)}, u32[]{:S(2)}) copy-start(bf16[128,1024]{1,0:T(8,128)(2,1)} %param.6) | copy-start | bytes 786436
  46.8 33.8 %all-to-all-start.1 = ((bf16[32,1,64]{2,1,0:T(2,128)(2,1)}), bf16[32,1,64]{2,1,0:T(2,128)(2,1)S(1)}, u32[]{:S(2)}, u32[]{:S(2)}) async-start(bf16[32,1,64]{2,1,0:T(2,128)(2,1)} %all_to_all.20), calls=%async_computation.1 | async-start | bytes 32768 | tf_op jit(solution)/shard_map/all_to_all | solution.py:56
  55.5 9.7 %copy-start.1 = (bf16[128,1024]{1,0:T(8,128)(2,1)S(1)}, bf16[128,1024]{1,0:T(8,128)(2,1)}, u32[]{:S(2)}) copy-start(bf16[128,1024]{1,0:T(8,128)(2,1)} %param.5) | copy-start | bytes 786436
  139.0 55.2 %all-to-all-start = ((bf16[32,64,1024]{2,1,0:T(8,128)(2,1)}), bf16[32,64,1024]{2,1,0:T(8,128)(2,1)}, u32[]{:S(2)}, u32[]{:S(2)}) async-start(bf16[32,64,1024]{2,1,0:T(8,128)(2,1)} %get-tuple-element.13), calls=%async_computation | async-start | bytes 8388608 | tf_op jit(solution)/shard_map/all_to_all | solution.py:55
  143.8 166.1 %reduce-scatter.2.cloned.1.call-start = ((), (), s32[]{:S(2)}) async-start(), calls=%async_computation.5 | async-start | bytes 9437184 | tf_op jit(solution)/shard_map/reduce_scatter | solution.py:69
  194.2 12.5 %copy-start.2 = (bf16[32,64,1024]{2,1,0:T(8,128)(2,1)S(1)}, bf16[32,64,1024]{2,1,0:T(8,128)(2,1)}, u32[]{:S(2)}) copy-start(bf16[32,64,1024]{2,1,0:T(8,128)(2,1)} %all_to_all.25) | copy-start | bytes 12582916
  204.7 2.0 copy-start.3
  224.0 58.3 %all-to-all-start.3 = ((bf16[32,64,1024]{2,1,0:T(8,128)(2,1)}), bf16[32,64,1024]{2,1,0:T(8,128)(2,1)}, u32[]{:S(2)}, u32[]{:S(2)}) async-start(bf16[32,64,1024]{2,1,0:T(8,128)(2,1)} %bitcast.68), calls=%async_computation.3 | async-start | bytes 8388608 | tf_op jit(solution)/shard_map/all_to_all | solution.py:62
Sparse Core Ops, SparseCore 0:
  213.7 96.2 reduce-scatter.1
where the time goes:
time: 319 us
  waiting for transfers between devices  118 us (37%)
  blocking collectives  58.4 us (18%)
  local copies, waits for them, and re-layouts  54.5 us (17%)
  other arithmetic  27 us (8%)
  matrix products  25.3 us (8%)
  starting transfers between devices  21.7 us (7%)
  between operations  14.2 us (4%)
    all_to_all x1, blocking collectives, local(): lax.all_to_all(send_z, 'expert', split_axis=0, concat_axis=0, tiled=True)  58.4 us
    all_to_all x1, waiting for transfers between devices, local(): lax.all_to_all(back.reshape(groups, width, rank), 'expert', split_axis=0,...  50.2 us
    all_to_all x1, waiting for transfers between devices, local(): lax.all_to_all(send_r, 'expert', split_axis=0, concat_axis=0, tiled=True)  50 us
    another operation x3, other arithmetic  18.2 us
    reduce_scatter x1, waiting for transfers between devices, local(): core_grad = lax.psum_scatter(term, 'dp', scatter_dimension=0, tiled=True)  17.7 us
    gather x1, local copies, waits for them, and re-layouts, local(): gates.reshape(pairs)[picks]  13.1 us
    dot_general x1, matrix products, expert_work(): jnp.einsum('slcr,lrq->slcq', sent_z, cores, preferred_element_type=jnp.fl...  10.5 us
    gather x1, local copies, waits for them, and re-layouts, local(): hidden_in[picks // topk]  9.65 us
  transfers between devices with their start and end apart: 4, of which 3 were waited for; matrix products, arithmetic and copies ran while one was open for 14% of the time, Pallas kernels for 0%

commit v1 on v0

v1 whole, which is shorter than its diff:
```python
import jax
import jax.numpy as jnp
from jax import lax
from jax.experimental import pallas as pl
from jax.experimental.pallas import tpu as pltpu
from jax.sharding import PartitionSpec as P

MESH = pl.DeviceIdType.MESH
F32 = jnp.float32
BF16 = jnp.bfloat16
NZ, NY, NX = 8, 4, 4
CQ = 256
NQ = 4
TOK = 128
CAP = 32
NS = NY * NX
ROWS = NS * CAP


def when(cond, fn):
    if isinstance(cond, bool):
        if cond:
            fn()
    else:
        pl.when(cond)(fn)


def cols(i):
    if isinstance(i, int):
        return pl.ds(i * CQ, CQ)
    return pl.ds(pl.multiple_of(i * CQ, CQ), CQ)


def body(
    h_ref, r_ref, meta_ref, cores_ref,
    rig_ref, cg_ref,
    ag, mb, core, zc, st, gs, lw, zct, bk, sel, selt, gc, asg, code, gts,
    z1, zs1, z2p, z2, z3, z4, rs1, rs2, rs3, rs4,
    core_sem, ag_s, ag_r, mt_s, mt_r, d2_s, d2_r, z_s, z_r, rs_s, rs_r,
):
    z = lax.axis_index("dp")
    ei = lax.axis_index("expert")
    c = lax.rem(ei, 2)
    x = lax.rem(lax.div(ei, 2), NX)
    y = lax.div(ei, 2 * NX)

    def wx(v):
        return lax.rem(v + NX, NX)

    def wz(v):
        return lax.rem(v + NZ, NZ)

    def dev(zz, yy, xx, cc):
        return (zz, (yy * NX + xx) * 2 + cc)

    def to_x(s):
        return dev(z, y, wx(x + s), c)

    def to_y(s):
        return dev(z, wx(y + s), x, c)

    def to_z(s):
        return dev(wz(z + s), y, x, c)

    twin = dev(z, y, x, 1 - c)

    def rcopy(src, dst, ssem, rsem, device):
        return pltpu.make_async_remote_copy(
            src_ref=src, dst_ref=dst, send_sem=ssem, recv_sem=rsem,
            device_id=device, device_id_type=MESH,
        )

    barrier = pltpu.get_barrier_semaphore()
    for device in (twin, to_x(1), to_x(-1), to_y(1), to_y(-1), to_z(1), to_z(-1)):
        pl.semaphore_signal(barrier, inc=1, device_id=device, device_id_type=MESH)
    core_copy = pltpu.make_async_copy(cores_ref, core, core_sem)
    core_copy.start()
    for n in range(NQ):
        ag[n, y, x] = h_ref[:, n * CQ:(n + 1) * CQ]
        ag[NQ + n, y, x] = r_ref[:, n * CQ:(n + 1) * CQ]
    mb[0, y, x] = meta_ref[...]
    pl.semaphore_wait(barrier, 7)

    SIDES = ((0, 1), (0, -1), (1, 1), (1, -1))

    def ag_msg(n, kind, half, s):
        o = half * 64
        whole = pl.ds(o, 64)
        part = pl.ds(o + (0 if s > 0 else 32), 32)
        if kind == 0:
            ref = ag.at[n, y, x, whole]
        elif kind == 1:
            ref = ag.at[n, y, wx(x - s), part] if half == 0 else ag.at[n, wx(y - s), x, part]
        elif kind == 2:
            ref = ag.at[n, y, :, whole] if half == 0 else ag.at[n, :, x, whole]
        else:
            ref = ag.at[n, wx(y - s), :, part] if half == 0 else ag.at[n, :, wx(x - s), part]
        along_x = (half == 0) == (kind < 2)
        k = kind * 4 + half * 2 + (0 if s > 0 else 1)
        return rcopy(ref, ref, ag_s.at[n, k], ag_r.at[n, k], to_x(s) if along_x else to_y(s))

    def ag_own(n):
        for half, s in SIDES:
            ag_msg(n, 0, half, s).start()

    def ag_a(n):
        for half, s in SIDES:
            ag_msg(n, 0, half, s).wait_recv()
            ag_msg(n, 1, half, s).start()

    def ag_b(n):
        for half in (0, 1):
            for s in (1, -1):
                ag_msg(n, 1, half, s).wait_recv()
            for s in (1, -1):
                ag_msg(n, 2, half, s).start()

    def ag_c(n):
        for half, s in SIDES:
            ag_msg(n, 2, half, s).wait_recv()
            ag_msg(n, 3, half, s).start()

    def ag_d(n):
        for half, s in SIDES:
            ag_msg(n, 3, half, s).wait_recv()

    def mt_msg(k):
        if k < 2:
            ref, device = mb.at[0, y, x], to_x(1 if k == 0 else -1)
        elif k == 2:
            ref, device = mb.at[0, y, wx(x - 1)], to_x(1)
        elif k < 5:
            ref, device = mb.at[0, y], to_y(1 if k == 3 else -1)
        elif k == 5:
            ref, device = mb.at[0, wx(y - 1)], to_y(1)
        else:
            return rcopy(mb.at[0], mb.at[1], mt_s.at[k], mt_r.at[k], twin)
        return rcopy(ref, ref, mt_s.at[k], mt_r.at[k], device)

    def d2_msg(n):
        return rcopy(st.at[n], zc.at[n, 1], d2_s.at[n], d2_r.at[n], twin)

    def d2_back(b):
        k = 2 * NQ + b
        return rcopy(st.at[b], bk.at[b, pl.ds(2, 2)], d2_s.at[k], d2_r.at[k], twin)

    def build_slots():
        first = (y * NX + x) * 4
        names = []
        for o in range(4):
            e = first + 2 * c + o if o < 2 else first + 2 * (1 - c) + (o - 2)
            names.append(e.astype(F32))

        def assign(i, carry):
            rel = lax.div(i, NS)
            s = lax.rem(i, NS)
            tile = mb[rel, lax.div(s, NX), lax.rem(s, NX)].astype(F32)
            ids, gates = tile[0:8], tile[8:16]
            marks, weights = [], []
            for o in range(4):
                eq = ids == names[o]
                marks.append(jnp.sum(jnp.where(eq, 1.0, 0.0), axis=0, keepdims=True))
                weights.append(jnp.sum(jnp.where(eq, gates, 0.0), axis=0, keepdims=True))
            pad = jnp.zeros((4, TOK), F32)
            at = pl.ds(pl.multiple_of(i * 8, 8), 8)
            asg[at, :] = jnp.concatenate(marks + [pad], axis=0)
            gts[at, :] = jnp.concatenate(weights + [pad], axis=0)
            return carry

        lax.fori_loop(0, 2 * NS, assign, 0)
        before = (
            lax.broadcasted_iota(jnp.int32, (TOK, TOK), 0)
            < lax.broadcasted_iota(jnp.int32, (TOK, TOK), 1)
        )
        upper = jnp.where(before, 1.0, 0.0).astype(BF16)
        marks = asg[...]
        places = jnp.dot(marks.astype(BF16), upper, preferred_element_type=F32)
        code[...] = jnp.where(marks > 0.5, places, -1.0)
        slot = lax.broadcasted_iota(jnp.int32, (CAP, TOK), 0).astype(F32)

        def choose(s, carry):
            rows = code[pl.ds(pl.multiple_of(s * 8, 8), 8), :]
            hot = jnp.concatenate(
                [
                    jnp.where(jnp.broadcast_to(rows[o:o + 1], (CAP, TOK)) == slot, 1.0, 0.0)
                    for o in range(4)
                ],
                axis=0,
            )
            sel[s] = hot.astype(BF16)
            selt[s] = hot.T.astype(BF16)
            return carry

        lax.fori_loop(0, NS, choose, 0)

        def weigh(i, carry):
            rel = lax.div(i, NS)
            s = lax.rem(i, NS)
            at = pl.ds(pl.multiple_of(i * 8, 8), 8)
            rows, weights = code[at, :], gts[at, :]
            for o in range(2):
                mine = jnp.where(
                    jnp.broadcast_to(rows[o:o + 1], (CAP, TOK)) == slot,
                    jnp.broadcast_to(weights[o:o + 1], (CAP, TOK)),
                    0.0,
                )
                total = jnp.sum(mine, axis=1, keepdims=True)
                gc[o, rel, pl.ds(pl.multiple_of(s * CAP, CAP), CAP), :] = jnp.broadcast_to(
                    total, (CAP, TOK)
                )
            return carry

        lax.fori_loop(0, 2 * NS, weigh, 0)

    def compact(n):
        def one(ys, carry):
            for xs in range(NX):
                s = ys * NX + xs
                rows = jnp.dot(sel[s], ag[n, ys, xs], preferred_element_type=F32).astype(BF16)
                zc[n, 0, 0, s] = rows[0:32]
                zc[n, 0, 1, s] = rows[32:64]
                st[n, 0, s] = rows[64:96]
                st[n, 1, s] = rows[96:128]
            return carry

        lax.fori_loop(0, NY, one, 0)

    def compute_h(n, first):
        compact(n)
        d2_msg(n).start()
        for rel in (0, 1):
            if rel == 1:
                d2_msg(n).wait_recv()
            at = pl.ds(rel * ROWS, ROWS)
            for e in (0, 1):
                rows = zc[n, rel, e].reshape(ROWS, CQ)
                zct[e, cols(n), at] = rows.T

                def grow(q, carry):
                    part = jnp.dot(
                        zc[n, rel, e].reshape(ROWS, CQ), core[e, cols(n), cols(q)],
                        preferred_element_type=F32,
                    )
                    gs[q, e, at, :] = part if first else gs[q, e, at, :] + part
                    return carry

                lax.fori_loop(0, NQ, grow, 0)

    def compute_r(q):
        n = NQ + q
        compact(n)
        d2_msg(n).start()
        step = 64
        for rel in (0, 1):
            if rel == 1:
                d2_msg(n).wait_recv()

            def lower(i, carry):
                for e in (0, 1):
                    at = pl.ds(pl.multiple_of(rel * ROWS + i * step, step), step)
                    up = gs[q, e, at, :]
                    r = zc[n, rel, e, pl.ds(i * 2, 2)].reshape(step, CQ).astype(F32)
                    g = gc[e, rel, pl.ds(pl.multiple_of(i * step, step), step), :]
                    g = jnp.concatenate([g, g], axis=1)
                    sig = jax.nn.sigmoid(up)
                    slope = sig * (1.0 + up * (1.0 - sig))
                    lw[q, e, at, :] = (r * g * slope).astype(BF16)
                return carry

            lax.fori_loop(0, ROWS // step, lower, 0)

        def term(i, carry):
            e, m = lax.div(i, 2), lax.rem(i, 2)
            at = pl.ds(pl.multiple_of(m * 512, 512), 512)
            gs[q, e, at, :] = jnp.dot(zct[e, at, :], lw[q, e], preferred_element_type=F32)
            return carry

        lax.fori_loop(0, 4, term, 0)

    def z_msg(q, k, s):
        i = 0 if s > 0 else 1
        src, dst = {
            1: (zs1, z1), 2: (z2p, z2), 3: (z2, z3), 4: (z3, z4),
        }[k]
        j = (k - 1) * 2 + i
        return rcopy(src.at[q, i], dst.at[q, i], z_s.at[q, j], z_r.at[q, j], to_z(s))

    def part_of(d):
        return pl.ds(pl.multiple_of(d * TOK, TOK), TOK)

    def z_step(k, q):
        if k == 5:
            total = gs[q, :, part_of(z), :]
            for i, s in ((0, 1), (1, -1)):
                z_msg(q, 4, s).wait_recv()
                total = total + z4[q, i].astype(F32)
            cg_ref[:, :, cols(q)] = total
            return
        for i, s in ((0, 1), (1, -1)):
            if k == 1:
                zs1[q, i] = gs[q, i, part_of(wz(z + 4)), :].astype(BF16)
            elif k == 2:
                z_msg(q, 1, s).wait_recv()
                at = part_of(wz(z + 3 * s))
                z2p[q, i, i] = (gs[q, i, at, :] + z1[q, i].astype(F32)).astype(BF16)
                z2p[q, i, 1 - i] = gs[q, 1 - i, at, :].astype(BF16)
            else:
                got = z2 if k == 3 else z3
                z_msg(q, k - 1, s).wait_recv()
                at = part_of(wz(z + (5 - k) * s))
                got[q, i] = (gs[q, :, at, :] + got[q, i].astype(F32)).astype(BF16)
            z_msg(q, k, s).start()

    def compute_b(b):
        for rel in (1, 0):
            def back(e, carry):
                total = None
                for q in range(NQ):
                    part = lax.dot_general(
                        lw[q, e, pl.ds(rel * ROWS, ROWS), :], core[e, cols(b), cols(q)],
                        (((1,), (1,)), ((), ())), preferred_element_type=F32,
                    )
                    total = part if total is None else total + part
                rows = total.astype(BF16).reshape(NS, CAP, CQ)
                if rel == 1:
                    st[b, e] = rows
                else:
                    bk[b, e] = rows
                return carry

            lax.fori_loop(0, 2, back, 0)
            if rel == 1:
                d2_back(b).start()
        d2_back(b).wait_recv()

        def scatter(ys, carry):
            for xs in range(NX):
                s = ys * NX + xs
                rows = bk[b, :, s].reshape(4 * CAP, CQ)
                ag[b, ys, xs] = jnp.dot(selt[s], rows, preferred_element_type=F32).astype(BF16)
            return carry

        lax.fori_loop(0, NY, scatter, 0)

    def rs_msg(b, k, half, s):
        i = 0 if s > 0 else 1
        o = half * 64
        whole = pl.ds(o, 64)
        part = pl.ds(o + 32 * i, 32)
        if k == 1:
            src = ag.at[b, wx(y + 2), :, part] if half == 0 else ag.at[b, :, wx(x + 2), part]
            dst = rs1
        elif k == 2:
            src = ag.at[b, wx(y + s), :, whole] if half == 0 else ag.at[b, :, wx(x + s), whole]
            dst = rs2
        elif k == 3:
            src = ag.at[b, y, wx(x + 2), part] if half == 0 else ag.at[b, wx(y + 2), x, part]
            dst = rs3
        else:
            src = ag.at[b, y, wx(x + s), whole] if half == 0 else ag.at[b, wx(y + s), x, whole]
            dst = rs4
        along_y = (half == 0) == (k < 3)
        j = (k - 1) * 4 + half * 2 + i
        return rcopy(
            src, dst.at[b, half, i], rs_s.at[b, j], rs_r.at[b, j], to_y(s) if along_y else to_x(s)
        )

    def rs_step(k, b):
        for half in (0, 1):
            o = half * 64
            whole = pl.ds(o, 64)
            if k == 2 or k == 4:
                for i, s in ((0, 1), (1, -1)):
                    rs_msg(b, k - 1, half, s).wait_recv()
                    part = pl.ds(o + 32 * i, 32)
                    if k == 4:
                        yy, xx = (y, wx(x + s)) if half == 0 else (wx(y + s), x)
                        ag[b, yy, xx, part] = (
                            ag[b, yy, xx, part].astype(F32) + rs3[b, half, i].astype(F32)
                        ).astype(BF16)
                    else:
                        def add(j, carry):
                            yy, xx = (wx(y + s), j) if half == 0 else (j, wx(x + s))
                            ag[b, yy, xx, part] = (
                                ag[b, yy, xx, part].astype(F32) + rs1[b, half, i, j].astype(F32)
                            ).astype(BF16)
                            return carry

                        lax.fori_loop(0, 4, add, 0)
                    rs_msg(b, k, half, s).start()
            elif k == 3:
                for s in (1, -1):
                    rs_msg(b, 2, half, s).wait_recv()

                def merge(j, carry):
                    yy, xx = (y, j) if half == 0 else (j, x)
                    ag[b, yy, xx, whole] = (
                        ag[b, yy, xx, whole].astype(F32)
                        + rs2[b, half, 0, j].astype(F32)
                        + rs2[b, half, 1, j].astype(F32)
                    ).astype(BF16)
                    return carry

                lax.fori_loop(0, 4, merge, 0)
                for s in (1, -1):
                    rs_msg(b, 3, half, s).start()
            elif k == 1:
                for s in (1, -1):
                    rs_msg(b, 1, half, s).start()
            else:
                for s in (1, -1):
                    rs_msg(b, 4, half, s).wait_recv()
                rig_ref[whole, cols(b)] = (
                    ag[b, y, x, whole].astype(F32)
                    + rs4[b, half, 0].astype(F32)
                    + rs4[b, half, 1].astype(F32)
                ).astype(BF16)

    mt_msg(0).start()
    mt_msg(1).start()
    ag_own(0)
    ag_own(1)
    mt_msg(0).wait_recv()
    mt_msg(2).start()
    mt_msg(1).wait_recv()
    ag_a(0)
    mt_msg(2).wait_recv()
    mt_msg(3).start()
    mt_msg(4).start()
    ag_b(0)
    ag_a(1)
    mt_msg(3).wait_recv()
    mt_msg(5).start()
    mt_msg(4).wait_recv()
    ag_b(1)

    def tick_comm(n, more, extra=None):
        ag_c(n)

        def ahead():
            ag_own(n + 2)
            ag_a(n + 2)
            ag_b(n + 2)

        when(more, ahead)
        if extra is not None:
            extra()
        ag_d(n)

    def meta_ready():
        mt_msg(5).wait_recv()
        mt_msg(6).start()
        mt_msg(6).wait_recv()
        build_slots()
        core_copy.wait()

    tick_comm(0, True, meta_ready)
    compute_h(0, True)

    def h_tick(n, carry):
        tick_comm(n, True)
        compute_h(n, False)
        return carry

    lax.fori_loop(1, NQ, h_tick, 0)

    def r_tick(q, carry):
        def chains():
            for k in (4, 3, 2):
                when(q >= k - 1, lambda k=k: z_step(k, q - (k - 1)))

        tick_comm(NQ + q, q < 2, chains)
        compute_r(q)
        z_step(1, q)
        return carry

    lax.fori_loop(0, NQ, r_tick, 0)

    def sent(n, carry):
        for kind in range(4):
            for half, s in SIDES:
                ag_msg(n, kind, half, s).wait_send()
        d2_msg(n).wait_send()
        return carry

    lax.fori_loop(0, 2 * NQ, sent, 0)

    def tail(t, carry):
        def fresh():
            compute_b(t)
            rs_step(1, t)

        when(t < NQ, fresh)
        for k in (5, 4, 3, 2):
            when((t >= k - 1) & (t < NQ + k - 1), lambda k=k: rs_step(k, t - (k - 1)))
        for k in (5, 4, 3, 2):
            when(t < k - 1, lambda k=k: z_step(k, t + 5 - k))
        return carry

    lax.fori_loop(0, NQ + 4, tail, 0)

    for k in range(7):
        mt_msg(k).wait_send()

    def flushed(q, carry):
        d2_back(q).wait_send()
        for k in range(1, 5):
            for s in (1, -1):
                z_msg(q, k, s).wait_send()
            for half, s in SIDES:
                rs_msg(q, k, half, s).wait_send()
        return carry

    lax.fori_loop(0, NQ, flushed, 0)


def local(hidden_in, rank_grad, gates, expert_ids, cores):
    meta = jnp.concatenate([expert_ids.T.astype(BF16), gates.T], axis=0)
    vmem = pl.BlockSpec(memory_space=pltpu.VMEM)
    dma = pltpu.SemaphoreType.DMA
    rig, cg = pl.pallas_call(
        body,
        out_shape=(
            jax.ShapeDtypeStruct((TOK, NQ * CQ), BF16),
            jax.ShapeDtypeStruct((2, TOK, NQ * CQ), F32),
        ),
        in_specs=[vmem, vmem, vmem, pl.BlockSpec(memory_space=pl.ANY)],
        out_specs=(vmem, vmem),
        scratch_shapes=[
            pltpu.VMEM((2 * NQ, NY, NX, TOK, CQ), BF16),
            pltpu.VMEM((2, NY, NX, 16, TOK), BF16),
            pltpu.VMEM((2, NQ * CQ, NQ * CQ), BF16),
            pltpu.VMEM((2 * NQ, 2, 2, NS, CAP, CQ), BF16),
            pltpu.VMEM((2 * NQ, 2, NS, CAP, CQ), BF16),
            pltpu.VMEM((NQ, 2, 2 * ROWS, CQ), F32),
            pltpu.VMEM((NQ, 2, 2 * ROWS, CQ), BF16),
            pltpu.VMEM((2, NQ * CQ, 2 * ROWS), BF16),
            pltpu.VMEM((NQ, 4, NS, CAP, CQ), BF16),
            pltpu.VMEM((NS, 4 * CAP, TOK), BF16),
            pltpu.VMEM((NS, TOK, 4 * CAP), BF16),
            pltpu.VMEM((2, 2, ROWS, TOK), F32),
            pltpu.VMEM((2 * NS * 8, TOK), F32),
            pltpu.VMEM((2 * NS * 8, TOK), F32),
            pltpu.VMEM((2 * NS * 8, TOK), F32),
            pltpu.VMEM((NQ, 2, TOK, CQ), BF16),
            pltpu.VMEM((NQ, 2, TOK, CQ), BF16),
            pltpu.VMEM((NQ, 2, 2, TOK, CQ), BF16),
            pltpu.VMEM((NQ, 2, 2, TOK, CQ), BF16),
            pltpu.VMEM((NQ, 2, 2, TOK, CQ), BF16),
            pltpu.VMEM((NQ, 2, 2, TOK, CQ), BF16),
            pltpu.VMEM((NQ, 2, 2, 4, 32, CQ), BF16),
            pltpu.VMEM((NQ, 2, 2, 4, 64, CQ), BF16),
            pltpu.VMEM((NQ, 2, 2, 32, CQ), BF16),
            pltpu.VMEM((NQ, 2, 2, 64, CQ), BF16),
            dma, dma((2 * NQ, 16)), dma((2 * NQ, 16)), dma((7,)), dma((7,)),
            dma((3 * NQ,)), dma((3 * NQ,)), dma((NQ, 8)), dma((NQ, 8)),
            dma((NQ, 16)), dma((NQ, 16)),
        ],
        compiler_params=pltpu.CompilerParams(
            collective_id=0, has_side_effects=True, vmem_limit_bytes=62 * 1024 * 1024
        ),
        cost_estimate=pl.CostEstimate(
            flops=14_000_000_000, bytes_accessed=8_000_000, transcendentals=2_000_000
        ),
        name="moe_core_backward",
    )(hidden_in, rank_grad, meta, cores)
    return rig, jnp.transpose(cg, (1, 0, 2))


def solution(mesh):
    in_specs = (
        P(("dp", "expert"), None),
        P(("dp", "expert"), None),
        P(("dp", "expert"), None),
        P(("dp", "expert"), None),
        P("expert", None, None),
    )
    out_specs = (P(("dp", "expert"), None), P("dp", "expert", None))
    return jax.shard_map(local, mesh=mesh, in_specs=in_specs, out_specs=out_specs, check_vma=False)
```

time: 319 us -> 181 us (0.57)
  Pallas kernels: 0 us -> 173 us
  waiting for transfers between devices: 118 us -> 0 us
  blocking collectives: 58.4 us -> 0 us
  local copies, waits for them, and re-layouts: 54.5 us -> 4.67 us
  matrix products: 25.3 us -> 0 us
  other arithmetic: 27 us -> 1.97 us
  starting transfers between devices: 21.7 us -> 0 us
  between operations: 14.2 us -> 0.64 us
    pallas_call x0 -> x1, Pallas kernels: none -> 173 us  [local(): pl.pallas_call(body, out_shape=(jax.ShapeDtypeStruct((TOK, NQ * CQ), BF16...]
    all_to_all x3 -> x0, waiting for transfers between devices: 100 us -> none  [the longest x1 50.2 us: local(): lax.all_to_all(back.reshape(groups, width, rank), 'expert', split_axis=0,...]
    all_to_all x1 -> x0, blocking collectives: 58.4 us -> none  [local(): lax.all_to_all(send_z, 'expert', split_axis=0, concat_axis=0, tiled=True)]
    gather x4 -> x0, local copies, waits for them, and re-layouts: 40.1 us -> none  [the longest x1 13.1 us: local(): gates.reshape(pairs)[picks]]
    dot_general x3 -> x0, matrix products: 25.3 us -> none  [the longest x1 10.5 us: expert_work(): jnp.einsum('slcr,lrq->slcq', sent_z, cores, preferred_element_type=jnp.fl...]
    all_to_all x3 -> x0, starting transfers between devices: 21.5 us -> none  [the longest x1 8.59 us: local(): lax.all_to_all(send_g, 'expert', split_axis=0, concat_axis=0, tiled=True)]
    another operation x3 -> x0, other arithmetic: 18.2 us -> none
    reduce_scatter x1 -> x0, waiting for transfers between devices: 17.7 us -> none  [local(): core_grad = lax.psum_scatter(term, 'dp', scatter_dimension=0, tiled=True)]
  transfers between devices with their start and end apart: 4 -> 0, of which waited for: 3 -> 0; matrix products, arithmetic and copies ran while one was open for 14% -> 0% of each run, Pallas kernels for 0% -> 0%
where the time goes in v1:
time: 181 us
  Pallas kernels  173 us (96%)
  local copies, waits for them, and re-layouts  4.67 us (3%)
  other arithmetic  1.97 us (1%)
    pallas_call x1, Pallas kernels, local(): pl.pallas_call(body, out_shape=(jax.ShapeDtypeStruct((TOK, NQ * CQ), BF16...  173 us
    unnamed x2, local copies, waits for them, and re-layouts  4.67 us

profile of v1, /device:TPU:1, one launch (start us, length us, event | category | flops | bytes accessed | tf_op | source)
XLA Modules:
  0.0 180.8 jit_solution(11596622687248840569)
XLA Ops:
  0.6 0.7 convert_bitcast_fusion
  1.3 1.3 pad_maximum_fusion.meta_ref
  2.6 173.5 %moe_core_backward.1 = (bf16[128,1024]{1,0:T(8,128)(2,1)}, f32[2,128,1024]{2,1,0:T(8,128)}) custom-call(bf16[128,1024]{1,0:T(8,128)(2,1)} %h_ref.1, bf16[128,1024]{1,0:T(8,128)(2,1)} %r_ref.1, bf16[16,128]{1,0:T(8,128)(2,1)} %pad_maximum_fusion.meta_ref, bf16[2,1024,1024]{2,1,0:T(8,128)(2,1)} %cores_ref.1), custom_call_target="tpu_custom_call" | custom-call | flops 14000000000 | bytes 8000000 | tf_op jit(solution)/shard_map/moe_core_backward/pallas_call | solution.py:521
  176.1 3.0 %copy.7 = f32[128,2,1024]{2,1,0:T(2,128)} copy(f32[128,2,1024]{2,0,1:T(8,128)} %bitcast.4) | data formatting | bytes 2097152
  179.1 1.7 copy.9

commit v2 on v1

--- a/solution.py
+++ b/solution.py
@@ -35,8 +35,8 @@
     h_ref, r_ref, meta_ref, cores_ref,
     rig_ref, cg_ref,
     ag, mb, core, zc, st, gs, lw, zct, bk, sel, selt, gc, asg, code, gts,
-    z1, zs1, z2p, z2, z3, z4, rs1, rs2, rs3, rs4,
-    core_sem, ag_s, ag_r, mt_s, mt_r, d2_s, d2_r, z_s, z_r, rs_s, rs_r,
+    z1, zs1, z2p, z2, z3, z4, rs1, rs2, rs3,
+    core_sem, p1_s, p1_r, ag_s, ag_r, mt_s, mt_r, d2_s, d2_r, z_s, z_r, rs_s, rs_r,
 ):
     z = lax.axis_index("dp")
     ei = lax.axis_index("expert")
@@ -71,68 +71,64 @@
         )
 
     barrier = pltpu.get_barrier_semaphore()
-    for device in (twin, to_x(1), to_x(-1), to_y(1), to_y(-1), to_z(1), to_z(-1)):
+    for device in (
+        twin, to_x(1), to_x(-1), to_x(2), to_y(1), to_y(-1), to_y(2), to_z(1), to_z(-1)
+    ):
         pl.semaphore_signal(barrier, inc=1, device_id=device, device_id_type=MESH)
     core_copy = pltpu.make_async_copy(cores_ref, core, core_sem)
     core_copy.start()
     for n in range(NQ):
         ag[n, y, x] = h_ref[:, n * CQ:(n + 1) * CQ]
-        ag[NQ + n, y, x] = r_ref[:, n * CQ:(n + 1) * CQ]
     mb[0, y, x] = meta_ref[...]
-    pl.semaphore_wait(barrier, 7)
+    pl.semaphore_wait(barrier, 9)
 
     SIDES = ((0, 1), (0, -1), (1, 1), (1, -1))
+    HOPS = (1, -1, 2)
+    GROUPS = ((0, 1), (1, NQ - 1), (NQ, NQ))
+
+    def near_msg(g, half, j):
+        lo, count = GROUPS[g]
+        ref = ag.at[pl.ds(lo, count), y, x, pl.ds(half * 64, 64)]
+        k = half * 3 + j
+        device = to_x(HOPS[j]) if half == 0 else to_y(HOPS[j])
+        return rcopy(ref, ref, p1_s.at[g, k], p1_r.at[g, k], device)
+
+    def near(g, act):
+        for half in (0, 1):
+            for j in range(3):
+                getattr(near_msg(g, half, j), act)()
 
     def ag_msg(n, kind, half, s):
         o = half * 64
         whole = pl.ds(o, 64)
         part = pl.ds(o + (0 if s > 0 else 32), 32)
         if kind == 0:
-            ref = ag.at[n, y, x, whole]
-        elif kind == 1:
-            ref = ag.at[n, y, wx(x - s), part] if half == 0 else ag.at[n, wx(y - s), x, part]
-        elif kind == 2:
             ref = ag.at[n, y, :, whole] if half == 0 else ag.at[n, :, x, whole]
         else:
             ref = ag.at[n, wx(y - s), :, part] if half == 0 else ag.at[n, :, wx(x - s), part]
-        along_x = (half == 0) == (kind < 2)
         k = kind * 4 + half * 2 + (0 if s > 0 else 1)
-        return rcopy(ref, ref, ag_s.at[n, k], ag_r.at[n, k], to_x(s) if along_x else to_y(s))
+        return rcopy(
+            ref, ref, ag_s.at[n, k], ag_r.at[n, k], to_y(s) if half == 0 else to_x(s)
+        )
 
     def ag_own(n):
         for half, s in SIDES:
             ag_msg(n, 0, half, s).start()
 
-    def ag_a(n):
+    def ag_on(n):
         for half, s in SIDES:
             ag_msg(n, 0, half, s).wait_recv()
             ag_msg(n, 1, half, s).start()
 
-    def ag_b(n):
-        for half in (0, 1):
-            for s in (1, -1):
-                ag_msg(n, 1, half, s).wait_recv()
-            for s in (1, -1):
-                ag_msg(n, 2, half, s).start()
-
-    def ag_c(n):
+    def ag_done(n):
         for half, s in SIDES:
-            ag_msg(n, 2, half, s).wait_recv()
-            ag_msg(n, 3, half, s).start()
-
-    def ag_d(n):
-        for half, s in SIDES:
-            ag_msg(n, 3, half, s).wait_recv()
+            ag_msg(n, 1, half, s).wait_recv()
 
     def mt_msg(k):
-        if k < 2:
-            ref, device = mb.at[0, y, x], to_x(1 if k == 0 else -1)
-        elif k == 2:
-            ref, device = mb.at[0, y, wx(x - 1)], to_x(1)
-        elif k < 5:
-            ref, device = mb.at[0, y], to_y(1 if k == 3 else -1)
-        elif k == 5:
-            ref, device = mb.at[0, wx(y - 1)], to_y(1)
+        if k < 3:
+            ref, device = mb.at[0, y, x], to_x(HOPS[k])
+        elif k < 6:
+            ref, device = mb.at[0, y], to_y(HOPS[k - 3])
         else:
             return rcopy(mb.at[0], mb.at[1], mt_s.at[k], mt_r.at[k], twin)
         return rcopy(ref, ref, mt_s.at[k], mt_r.at[k], device)
@@ -192,6 +188,9 @@
             return carry
 
         lax.fori_loop(0, NS, choose, 0)
+
+    def build_gates():
+        slot = lax.broadcasted_iota(jnp.int32, (CAP, TOK), 0).astype(F32)
 
         def weigh(i, carry):
             rel = lax.div(i, NS)
@@ -225,26 +224,35 @@
 
         lax.fori_loop(0, NY, one, 0)
 
-    def compute_h(n, first):
+    def turn(n, rel):
+        for e in (0, 1):
+            zct[e, cols(n), pl.ds(rel * ROWS, ROWS)] = zc[n, rel, e].reshape(ROWS, CQ).T
+
+    def compute_h(n):
         compact(n)
         d2_msg(n).start()
-        for rel in (0, 1):
-            if rel == 1:
-                d2_msg(n).wait_recv()
-            at = pl.ds(rel * ROWS, ROWS)
-            for e in (0, 1):
-                rows = zc[n, rel, e].reshape(ROWS, CQ)
-                zct[e, cols(n), at] = rows.T
-
-                def grow(q, carry):
-                    part = jnp.dot(
-                        zc[n, rel, e].reshape(ROWS, CQ), core[e, cols(n), cols(q)],
-                        preferred_element_type=F32,
-                    )
-                    gs[q, e, at, :] = part if first else gs[q, e, at, :] + part
-                    return carry
-
-                lax.fori_loop(0, NQ, grow, 0)
+        turn(n, 0)
+
+        def other():
+            d2_msg(n - 1).wait_recv()
+            turn(n - 1, 1)
+
+        when(n >= 1, other)
+
+    def compute_upper(q):
+        def one(i, carry):
+            e, rel = lax.div(i, 2), lax.rem(i, 2)
+            total = None
+            for n in range(NQ):
+                part = jnp.dot(
+                    zc[n, rel, e].reshape(ROWS, CQ), core[e, cols(n), cols(q)],
+                    preferred_element_type=F32,
+                )
+                total = part if total is None else total + part
+            gs[q, e, pl.ds(pl.multiple_of(rel * ROWS, ROWS), ROWS), :] = total
+            return carry
+
+        lax.fori_loop(0, 4, one, 0)
 
     def compute_r(q):
         n = NQ + q
@@ -350,44 +358,44 @@
         if k == 1:
             src = ag.at[b, wx(y + 2), :, part] if half == 0 else ag.at[b, :, wx(x + 2), part]
             dst = rs1
-        elif k == 2:
+        else:
             src = ag.at[b, wx(y + s), :, whole] if half == 0 else ag.at[b, :, wx(x + s), whole]
             dst = rs2
-        elif k == 3:
-            src = ag.at[b, y, wx(x + 2), part] if half == 0 else ag.at[b, wx(y + 2), x, part]
-            dst = rs3
-        else:
-            src = ag.at[b, y, wx(x + s), whole] if half == 0 else ag.at[b, wx(y + s), x, whole]
-            dst = rs4
-        along_y = (half == 0) == (k < 3)
         j = (k - 1) * 4 + half * 2 + i
         return rcopy(
-            src, dst.at[b, half, i], rs_s.at[b, j], rs_r.at[b, j], to_y(s) if along_y else to_x(s)
+            src, dst.at[b, half, i], rs_s.at[b, j], rs_r.at[b, j], to_y(s) if half == 0 else to_x(s)
+        )
+
+    def last_msg(b, half, j):
+        whole = pl.ds(half * 64, 64)
+        s = HOPS[j]
+        src = ag.at[b, y, wx(x + s), whole] if half == 0 else ag.at[b, wx(y + s), x, whole]
+        k = 8 + half * 3 + j
+        return rcopy(
+            src, rs3.at[b, half, j], rs_s.at[b, k], rs_r.at[b, k], to_x(s) if half == 0 else to_y(s)
         )
 
     def rs_step(k, b):
         for half in (0, 1):
             o = half * 64
             whole = pl.ds(o, 64)
-            if k == 2 or k == 4:
+            if k == 1:
+                for s in (1, -1):
+                    rs_msg(b, 1, half, s).start()
+            elif k == 2:
                 for i, s in ((0, 1), (1, -1)):
-                    rs_msg(b, k - 1, half, s).wait_recv()
+                    rs_msg(b, 1, half, s).wait_recv()
                     part = pl.ds(o + 32 * i, 32)
-                    if k == 4:
-                        yy, xx = (y, wx(x + s)) if half == 0 else (wx(y + s), x)
+
+                    def add(j, carry):
+                        yy, xx = (wx(y + s), j) if half == 0 else (j, wx(x + s))
                         ag[b, yy, xx, part] = (
-                            ag[b, yy, xx, part].astype(F32) + rs3[b, half, i].astype(F32)
+                            ag[b, yy, xx, part].astype(F32) + rs1[b, half, i, j].astype(F32)
                         ).astype(BF16)
-                    else:
-                        def add(j, carry):
-                            yy, xx = (wx(y + s), j) if half == 0 else (j, wx(x + s))
-                            ag[b, yy, xx, part] = (
-                                ag[b, yy, xx, part].astype(F32) + rs1[b, half, i, j].astype(F32)
-                            ).astype(BF16)
-                            return carry
-
-                        lax.fori_loop(0, 4, add, 0)
-                    rs_msg(b, k, half, s).start()
+                        return carry
+
+                    lax.fori_loop(0, 4, add, 0)
+                    rs_msg(b, 2, half, s).start()
             elif k == 3:
                 for s in (1, -1):
                     rs_msg(b, 2, half, s).wait_recv()
@@ -402,74 +410,60 @@
                     return carry
 
                 lax.fori_loop(0, 4, merge, 0)
-                for s in (1, -1):
-                    rs_msg(b, 3, half, s).start()
-            elif k == 1:
-                for s in (1, -1):
-                    rs_msg(b, 1, half, s).start()
+                for j in range(3):
+                    last_msg(b, half, j).start()
             else:
-                for s in (1, -1):
-                    rs_msg(b, 4, half, s).wait_recv()
-                rig_ref[whole, cols(b)] = (
-                    ag[b, y, x, whole].astype(F32)
-                    + rs4[b, half, 0].astype(F32)
-                    + rs4[b, half, 1].astype(F32)
-                ).astype(BF16)
-
-    mt_msg(0).start()
-    mt_msg(1).start()
+                total = ag[b, y, x, whole].astype(F32)
+                for j in range(3):
+                    last_msg(b, half, j).wait_recv()
+                    total = total + rs3[b, half, j].astype(F32)
+                rig_ref[whole, cols(b)] = total.astype(BF16)
+
+    near(0, "start")
+    for k in range(3):
+        mt_msg(k).start()
+    near(1, "start")
+    for n in range(NQ):
+        ag[NQ + n, y, x] = r_ref[:, n * CQ:(n + 1) * CQ]
+    for k in range(3):
+        mt_msg(k).wait_recv()
+    for k in range(3, 6):
+        mt_msg(k).start()
+    near(0, "wait_recv")
     ag_own(0)
+    near(1, "wait_recv")
     ag_own(1)
-    mt_msg(0).wait_recv()
-    mt_msg(2).start()
-    mt_msg(1).wait_recv()
-    ag_a(0)
-    mt_msg(2).wait_recv()
-    mt_msg(3).start()
-    mt_msg(4).start()
-    ag_b(0)
-    ag_a(1)
-    mt_msg(3).wait_recv()
-    mt_msg(5).start()
-    mt_msg(4).wait_recv()
-    ag_b(1)
-
-    def tick_comm(n, more, extra=None):
-        ag_c(n)
-
-        def ahead():
-            ag_own(n + 2)
-            ag_a(n + 2)
-            ag_b(n + 2)
-
-        when(more, ahead)
-        if extra is not None:
-            extra()
-        ag_d(n)
-
-    def meta_ready():
-        mt_msg(5).wait_recv()
-        mt_msg(6).start()
-        mt_msg(6).wait_recv()
-        build_slots()
-        core_copy.wait()
-
-    tick_comm(0, True, meta_ready)
-    compute_h(0, True)
+    for k in range(3, 6):
+        mt_msg(k).wait_recv()
+    mt_msg(6).start()
+    mt_msg(6).wait_recv()
+    build_slots()
+    core_copy.wait()
+    ag_on(0)
+    ag_own(2)
+    near(2, "start")
 
     def h_tick(n, carry):
-        tick_comm(n, True)
-        compute_h(n, False)
+        ag_on(n)
+        when(n == 2, lambda: near(2, "wait_recv"))
+        ag_own(n + 2)
+        ag_done(n - 1)
+        compute_h(n - 1)
         return carry
 
-    lax.fori_loop(1, NQ, h_tick, 0)
+    lax.fori_loop(1, NQ + 1, h_tick, 0)
+    build_gates()
+    d2_msg(NQ - 1).wait_recv()
+    turn(NQ - 1, 1)
 
     def r_tick(q, carry):
-        def chains():
-            for k in (4, 3, 2):
-                when(q >= k - 1, lambda k=k: z_step(k, q - (k - 1)))
-
-        tick_comm(NQ + q, q < 2, chains)
+        n = NQ + 1 + q
+        when(q < NQ - 1, lambda: ag_on(n))
+        when(q < 1, lambda: ag_own(n + 2))
+        compute_upper(q)
+        for k in (4, 3, 2):
+            when(q >= k - 1, lambda k=k: z_step(k, q - (k - 1)))
+        ag_done(n - 1)
         compute_r(q)
         z_step(1, q)
         return carry
@@ -477,13 +471,15 @@
     lax.fori_loop(0, NQ, r_tick, 0)
 
     def sent(n, carry):
-        for kind in range(4):
+        for kind in range(2):
             for half, s in SIDES:
                 ag_msg(n, kind, half, s).wait_send()
         d2_msg(n).wait_send()
         return carry
 
     lax.fori_loop(0, 2 * NQ, sent, 0)
+    for g in range(3):
+        near(g, "wait_send")
 
     def tail(t, carry):
         def fresh():
@@ -491,13 +487,13 @@
             rs_step(1, t)
 
         when(t < NQ, fresh)
-        for k in (5, 4, 3, 2):
+        for k in (4, 3, 2):
             when((t >= k - 1) & (t < NQ + k - 1), lambda k=k: rs_step(k, t - (k - 1)))
         for k in (5, 4, 3, 2):
             when(t < k - 1, lambda k=k: z_step(k, t + 5 - k))
         return carry
 
-    lax.fori_loop(0, NQ + 4, tail, 0)
+    lax.fori_loop(0, NQ + 3, tail, 0)
 
     for k in range(7):
         mt_msg(k).wait_send()
@@ -507,8 +503,12 @@
         for k in range(1, 5):
             for s in (1, -1):
                 z_msg(q, k, s).wait_send()
-            for half, s in SIDES:
+        for half, s in SIDES:
+            for k in (1, 2):
                 rs_msg(q, k, half, s).wait_send()
+        for half in (0, 1):
+            for j in range(3):
+                last_msg(q, half, j).wait_send()
         return carry
 
     lax.fori_loop(0, NQ, flushed, 0)
@@ -550,11 +550,10 @@
             pltpu.VMEM((NQ, 2, 2, TOK, CQ), BF16),
             pltpu.VMEM((NQ, 2, 2, 4, 32, CQ), BF16),
             pltpu.VMEM((NQ, 2, 2, 4, 64, CQ), BF16),
-            pltpu.VMEM((NQ, 2, 2, 32, CQ), BF16),
-            pltpu.VMEM((NQ, 2, 2, 64, CQ), BF16),
-            dma, dma((2 * NQ, 16)), dma((2 * NQ, 16)), dma((7,)), dma((7,)),
+            pltpu.VMEM((NQ, 2, 3, 64, CQ), BF16),
+            dma, dma((3, 6)), dma((3, 6)), dma((2 * NQ, 8)), dma((2 * NQ, 8)), dma((7,)), dma((7,)),
             dma((3 * NQ,)), dma((3 * NQ,)), dma((NQ, 8)), dma((NQ, 8)),
-            dma((NQ, 16)), dma((NQ, 16)),
+            dma((NQ, 14)), dma((NQ, 14)),
         ],
         compiler_params=pltpu.CompilerParams(
             collective_id=0, has_side_effects=True, vmem_limit_bytes=62 * 1024 * 1024

time: 181 us -> 138 us (0.76)
  Pallas kernels: 173 us -> 130 us
    pallas_call x1, Pallas kernels: 173 us -> 130 us  [local(): pl.pallas_call(body, out_shape=(jax.ShapeDtypeStruct((TOK, NQ * CQ), BF16...]
where the time goes in v2:
time: 138 us; the launch traced here: 137 us
  Pallas kernels  130 us (94%)
  local copies, waits for them, and re-layouts  4.67 us (3%)
  other arithmetic  1.97 us (1%)
    pallas_call x1, Pallas kernels, local(): pl.pallas_call(body, out_shape=(jax.ShapeDtypeStruct((TOK, NQ * CQ), BF16...  130 us
    unnamed x2, local copies, waits for them, and re-layouts  4.67 us

profile of v2, /device:TPU:1, one launch (start us, length us, event | category | flops | bytes accessed | tf_op | source)
XLA Modules:
  0.0 137.3 jit_solution(1722485955221223645)
XLA Ops:
  0.6 0.7 convert_bitcast_fusion
  1.3 1.3 pad_maximum_fusion.meta_ref
  2.6 130.0 %moe_core_backward.1 = (bf16[128,1024]{1,0:T(8,128)(2,1)}, f32[2,128,1024]{2,1,0:T(8,128)}) custom-call(bf16[128,1024]{1,0:T(8,128)(2,1)} %h_ref.1, bf16[128,1024]{1,0:T(8,128)(2,1)} %r_ref.1, bf16[16,128]{1,0:T(8,128)(2,1)} %pad_maximum_fusion.meta_ref, bf16[2,1024,1024]{2,1,0:T(8,128)(2,1)} %cores_ref.1), custom_call_target="tpu_custom_call" | custom-call | flops 14000000000 | bytes 8000000 | tf_op jit(solution)/shard_map/moe_core_backward/pallas_call | solution.py:521
  132.6 3.0 %copy.7 = f32[128,2,1024]{2,1,0:T(2,128)} copy(f32[128,2,1024]{2,0,1:T(8,128)} %bitcast.4) | data formatting | bytes 2097152
  135.7 1.7 %copy.9 = bf16[128,1024]{1,0:T(8,128)(2,1)} copy(bf16[128,1024]{1,0:T(8,128)(2,1)} %get-tuple-element.10) | data formatting | bytes 524288

commit v3 on v2

--- a/solution.py
+++ b/solution.py
@@ -17,6 +17,19 @@
 ROWS = NS * CAP
 
 
+ORDER = (
+    ("o", 5), ("u", 0), ("u", 1), ("o", 6), ("c", 0), ("k", 0), ("c", 1), ("o", 7), ("k", 1),
+    ("l", 0), ("t", 0), ("z1", 0), ("l", 1), ("t", 1), ("z1", 1), ("c", 2), ("z2", 0), ("c", 3),
+    ("u", 2), ("z2", 1), ("u", 3), ("k", 3), ("z3", 0), ("k", 2), ("l", 2), ("l", 3), ("b", 0),
+    ("a", 0), ("z3", 1), ("b", 1), ("a", 1), ("s", 0), ("r1", 0), ("z4", 0), ("t", 3),
+    ("z1", 3), ("z4", 1), ("s", 1), ("r1", 1), ("r2", 0), ("t", 2), ("z1", 2), ("z2", 3),
+    ("b", 2), ("r2", 1), ("a", 2), ("b", 3), ("r3", 0), ("z2", 2), ("s", 2), ("r1", 2),
+    ("a", 3), ("r3", 1), ("z3", 3), ("s", 3), ("r1", 3), ("r4", 0), ("z5", 0), ("r2", 2),
+    ("z3", 2), ("z5", 1), ("r4", 1), ("r2", 3), ("z4", 3), ("r3", 2), ("z4", 2), ("r3", 3),
+    ("z5", 3), ("r4", 2), ("z5", 2), ("r4", 3),
+)
+
+
 def when(cond, fn):
     if isinstance(cond, bool):
         if cond:
@@ -32,7 +45,7 @@
 
 
 def body(
-    h_ref, r_ref, meta_ref, cores_ref,
+    h_ref, r_ref, ids_ref, gates_ref, cores_ref,
     rig_ref, cg_ref,
     ag, mb, core, zc, st, gs, lw, zct, bk, sel, selt, gc, asg, code, gts,
     z1, zs1, z2p, z2, z3, z4, rs1, rs2, rs3,
@@ -79,7 +92,9 @@
     core_copy.start()
     for n in range(NQ):
         ag[n, y, x] = h_ref[:, n * CQ:(n + 1) * CQ]
-    mb[0, y, x] = meta_ref[...]
+    mb[0, y, x] = jnp.concatenate(
+        [ids_ref[...].astype(F32), gates_ref[...].astype(F32)], axis=0
+    ).astype(BF16)
     pl.semaphore_wait(barrier, 9)
 
     SIDES = ((0, 1), (0, -1), (1, 1), (1, -1))
@@ -140,16 +155,15 @@
         k = 2 * NQ + b
         return rcopy(st.at[b], bk.at[b, pl.ds(2, 2)], d2_s.at[k], d2_r.at[k], twin)
 
-    def build_slots():
+    def build_slots(rel):
         first = (y * NX + x) * 4
         names = []
         for o in range(4):
             e = first + 2 * c + o if o < 2 else first + 2 * (1 - c) + (o - 2)
             names.append(e.astype(F32))
 
-        def assign(i, carry):
-            rel = lax.div(i, NS)
-            s = lax.rem(i, NS)
+        def assign(s, carry):
+            i = rel * NS + s
             tile = mb[rel, lax.div(s, NX), lax.rem(s, NX)].astype(F32)
             ids, gates = tile[0:8], tile[8:16]
             marks, weights = [], []
@@ -163,15 +177,18 @@
             gts[at, :] = jnp.concatenate(weights + [pad], axis=0)
             return carry
 
-        lax.fori_loop(0, 2 * NS, assign, 0)
+        lax.fori_loop(0, NS, assign, 0)
         before = (
             lax.broadcasted_iota(jnp.int32, (TOK, TOK), 0)
             < lax.broadcasted_iota(jnp.int32, (TOK, TOK), 1)
         )
         upper = jnp.where(before, 1.0, 0.0).astype(BF16)
-        marks = asg[...]
+        rows = pl.ds(rel * NS * 8, NS * 8)
+        marks = asg[rows, :]
         places = jnp.dot(marks.astype(BF16), upper, preferred_element_type=F32)
-        code[...] = jnp.where(marks > 0.5, places, -1.0)
+        code[rows, :] = jnp.where(marks > 0.5, places, -1.0)
+        if rel == 1:
+            return
         slot = lax.broadcasted_iota(jnp.int32, (CAP, TOK), 0).astype(F32)
 
         def choose(s, carry):
@@ -242,41 +259,42 @@
     def compute_upper(q):
         def one(i, carry):
             e, rel = lax.div(i, 2), lax.rem(i, 2)
-            total = None
-            for n in range(NQ):
-                part = jnp.dot(
-                    zc[n, rel, e].reshape(ROWS, CQ), core[e, cols(n), cols(q)],
-                    preferred_element_type=F32,
-                )
-                total = part if total is None else total + part
-            gs[q, e, pl.ds(pl.multiple_of(rel * ROWS, ROWS), ROWS), :] = total
+            rows = jnp.concatenate(
+                [zc[n, rel, e].reshape(ROWS, CQ) for n in range(NQ)], axis=1
+            )
+            gs[q, e, pl.ds(pl.multiple_of(rel * ROWS, ROWS), ROWS), :] = jnp.dot(
+                rows, core[e, :, cols(q)], preferred_element_type=F32
+            )
             return carry
 
         lax.fori_loop(0, 4, one, 0)
 
-    def compute_r(q):
+    def gather_r(q):
+        ag_done(NQ + q)
+        compact(NQ + q)
+        d2_msg(NQ + q).start()
+
+    def lower_r(q, rel):
         n = NQ + q
-        compact(n)
-        d2_msg(n).start()
         step = 64
-        for rel in (0, 1):
-            if rel == 1:
-                d2_msg(n).wait_recv()
-
-            def lower(i, carry):
-                for e in (0, 1):
-                    at = pl.ds(pl.multiple_of(rel * ROWS + i * step, step), step)
-                    up = gs[q, e, at, :]
-                    r = zc[n, rel, e, pl.ds(i * 2, 2)].reshape(step, CQ).astype(F32)
-                    g = gc[e, rel, pl.ds(pl.multiple_of(i * step, step), step), :]
-                    g = jnp.concatenate([g, g], axis=1)
-                    sig = jax.nn.sigmoid(up)
-                    slope = sig * (1.0 + up * (1.0 - sig))
-                    lw[q, e, at, :] = (r * g * slope).astype(BF16)
-                return carry
-
-            lax.fori_loop(0, ROWS // step, lower, 0)
-
+        if rel == 1:
+            d2_msg(n).wait_recv()
+
+        def lower(i, carry):
+            for e in (0, 1):
+                at = pl.ds(pl.multiple_of(rel * ROWS + i * step, step), step)
+                up = gs[q, e, at, :]
+                r = zc[n, rel, e, pl.ds(i * 2, 2)].reshape(step, CQ).astype(F32)
+                g = gc[e, rel, pl.ds(pl.multiple_of(i * step, step), step), :]
+                g = jnp.concatenate([g, g], axis=1)
+                sig = jax.nn.sigmoid(up)
+                slope = sig * (1.0 + up * (1.0 - sig))
+                lw[q, e, at, :] = (r * g * slope).astype(BF16)
+            return carry
+
+        lax.fori_loop(0, ROWS // step, lower, 0)
+
+    def form_term(q):
         def term(i, carry):
             e, m = lax.div(i, 2), lax.rem(i, 2)
             at = pl.ds(pl.multiple_of(m * 512, 512), 512)
@@ -319,26 +337,27 @@
                 got[q, i] = (gs[q, :, at, :] + got[q, i].astype(F32)).astype(BF16)
             z_msg(q, k, s).start()
 
-    def compute_b(b):
-        for rel in (1, 0):
-            def back(e, carry):
-                total = None
-                for q in range(NQ):
-                    part = lax.dot_general(
-                        lw[q, e, pl.ds(rel * ROWS, ROWS), :], core[e, cols(b), cols(q)],
-                        (((1,), (1,)), ((), ())), preferred_element_type=F32,
-                    )
-                    total = part if total is None else total + part
-                rows = total.astype(BF16).reshape(NS, CAP, CQ)
-                if rel == 1:
-                    st[b, e] = rows
-                else:
-                    bk[b, e] = rows
-                return carry
-
-            lax.fori_loop(0, 2, back, 0)
+    def form_back(b, rel):
+        def back(e, carry):
+            rows = jnp.concatenate(
+                [lw[q, e, pl.ds(rel * ROWS, ROWS), :] for q in range(NQ)], axis=1
+            )
+            total = lax.dot_general(
+                rows, core[e, cols(b), :], (((1,), (1,)), ((), ())),
+                preferred_element_type=F32,
+            )
+            rows = total.astype(BF16).reshape(NS, CAP, CQ)
             if rel == 1:
-                d2_back(b).start()
+                st[b, e] = rows
+            else:
+                bk[b, e] = rows
+            return carry
+
+        lax.fori_loop(0, 2, back, 0)
+        if rel == 1:
+            d2_back(b).start()
+
+    def scatter_b(b):
         d2_back(b).wait_recv()
 
         def scatter(ys, carry):
@@ -436,8 +455,7 @@
     for k in range(3, 6):
         mt_msg(k).wait_recv()
     mt_msg(6).start()
-    mt_msg(6).wait_recv()
-    build_slots()
+    build_slots(0)
     core_copy.wait()
     ag_on(0)
     ag_own(2)
@@ -452,23 +470,11 @@
         return carry
 
     lax.fori_loop(1, NQ + 1, h_tick, 0)
+    mt_msg(6).wait_recv()
+    build_slots(1)
     build_gates()
     d2_msg(NQ - 1).wait_recv()
     turn(NQ - 1, 1)
-
-    def r_tick(q, carry):
-        n = NQ + 1 + q
-        when(q < NQ - 1, lambda: ag_on(n))
-        when(q < 1, lambda: ag_own(n + 2))
-        compute_upper(q)
-        for k in (4, 3, 2):
-            when(q >= k - 1, lambda k=k: z_step(k, q - (k - 1)))
-        ag_done(n - 1)
-        compute_r(q)
-        z_step(1, q)
-        return carry
-
-    lax.fori_loop(0, NQ, r_tick, 0)
 
     def sent(n, carry):
         for kind in range(2):
@@ -477,23 +483,34 @@
         d2_msg(n).wait_send()
         return carry
 
-    lax.fori_loop(0, 2 * NQ, sent, 0)
-    for g in range(3):
-        near(g, "wait_send")
-
-    def tail(t, carry):
-        def fresh():
-            compute_b(t)
-            rs_step(1, t)
-
-        when(t < NQ, fresh)
-        for k in (4, 3, 2):
-            when((t >= k - 1) & (t < NQ + k - 1), lambda k=k: rs_step(k, t - (k - 1)))
-        for k in (5, 4, 3, 2):
-            when(t < k - 1, lambda k=k: z_step(k, t + 5 - k))
-        return carry
-
-    lax.fori_loop(0, NQ + 3, tail, 0)
+    steps = {
+        "o": ag_on,
+        "u": compute_upper,
+        "c": gather_r,
+        "k": lambda q: lower_r(q, 0),
+        "l": lambda q: lower_r(q, 1),
+        "t": form_term,
+        "b": lambda b: form_back(b, 1),
+        "a": lambda b: form_back(b, 0),
+        "s": scatter_b,
+    }
+    cleared = False
+    for name, i in ORDER:
+        if name == "b" and not cleared:
+            lax.fori_loop(0, NQ, sent, 0)
+            near(0, "wait_send")
+            near(1, "wait_send")
+            cleared = True
+        if name[0] == "z":
+            z_step(int(name[1]), i)
+        elif name[0] == "r":
+            rs_step(int(name[1]), i)
+        else:
+            steps[name](i)
+        if name == "o" and i == NQ + 1:
+            ag_own(2 * NQ - 1)
+    lax.fori_loop(NQ, 2 * NQ, sent, 0)
+    near(2, "wait_send")
 
     for k in range(7):
         mt_msg(k).wait_send()
@@ -515,7 +532,6 @@
 
 
 def local(hidden_in, rank_grad, gates, expert_ids, cores):
-    meta = jnp.concatenate([expert_ids.T.astype(BF16), gates.T], axis=0)
     vmem = pl.BlockSpec(memory_space=pltpu.VMEM)
     dma = pltpu.SemaphoreType.DMA
     rig, cg = pl.pallas_call(
@@ -524,7 +540,7 @@
             jax.ShapeDtypeStruct((TOK, NQ * CQ), BF16),
             jax.ShapeDtypeStruct((2, TOK, NQ * CQ), F32),
         ),
-        in_specs=[vmem, vmem, vmem, pl.BlockSpec(memory_space=pl.ANY)],
+        in_specs=[vmem, vmem, vmem, vmem, pl.BlockSpec(memory_space=pl.ANY)],
         out_specs=(vmem, vmem),
         scratch_shapes=[
             pltpu.VMEM((2 * NQ, NY, NX, TOK, CQ), BF16),
@@ -562,7 +578,7 @@
             flops=14_000_000_000, bytes_accessed=8_000_000, transcendentals=2_000_000
         ),
         name="moe_core_backward",
-    )(hidden_in, rank_grad, meta, cores)
+    )(hidden_in, rank_grad, expert_ids.T, gates.T, cores)
     return rig, jnp.transpose(cg, (1, 0, 2))
 
 

time: 138 us -> 112 us (0.81)
  Pallas kernels: 130 us -> 105 us
  other arithmetic: 1.97 us -> 0 us
    pallas_call x1, Pallas kernels: 130 us -> 105 us  [local(): pl.pallas_call(body, out_shape=(jax.ShapeDtypeStruct((TOK, NQ * CQ), BF16...]
where the time goes in v3:
time: 112 us; the launch traced here: 111 us
  Pallas kernels  105 us (94%)
  local copies, waits for them, and re-layouts  4.67 us (4%)
    pallas_call x1, Pallas kernels, local(): pl.pallas_call(body, out_shape=(jax.ShapeDtypeStruct((TOK, NQ * CQ), BF16...  105 us
    unnamed x2, local copies, waits for them, and re-layouts  4.67 us

profile of v3, /device:TPU:1, one launch (start us, length us, event | category | flops | bytes accessed | tf_op | source)
XLA Modules:
  0.0 110.5 jit_solution(16605496385704224610)
XLA Ops:
  0.6 105.2 %moe_core_backward.1 = (bf16[128,1024]{1,0:T(8,128)(2,1)}, f32[2,128,1024]{2,1,0:T(8,128)}) custom-call(bf16[128,1024]{1,0:T(8,128)(2,1)} %h_ref.1, bf16[128,1024]{1,0:T(8,128)(2,1)} %r_ref.1, s32[8,128]{1,0:T(8,128)} %bitcast.4, bf16[8,128]{1,0:T(8,128)(2,1)} %bitcast.5, bf16[2,1024,1024]{2,1,0:T(8,128)(2,1)} %cores_ref.1), custom_call_target="tpu_custom_call" | custom-call | flops 14000000000 | bytes 8000000 | tf_op jit(solution)/shard_map/moe_core_backward/pallas_call | solution.py:537
  105.9 3.0 %copy.7 = f32[128,2,1024]{2,1,0:T(2,128)} copy(f32[128,2,1024]{2,0,1:T(8,128)} %bitcast.3) | data formatting | bytes 2097152
  108.9 1.7 %copy.9 = bf16[128,1024]{1,0:T(8,128)(2,1)} copy(bf16[128,1024]{1,0:T(8,128)(2,1)} %get-tuple-element.10) | data formatting | bytes 524288

commit v4 on v3

--- a/solution.py
+++ b/solution.py
@@ -18,15 +18,15 @@
 
 
 ORDER = (
-    ("o", 5), ("u", 0), ("u", 1), ("o", 6), ("c", 0), ("k", 0), ("c", 1), ("o", 7), ("k", 1),
-    ("l", 0), ("t", 0), ("z1", 0), ("l", 1), ("t", 1), ("z1", 1), ("c", 2), ("z2", 0), ("c", 3),
-    ("u", 2), ("z2", 1), ("u", 3), ("k", 3), ("z3", 0), ("k", 2), ("l", 2), ("l", 3), ("b", 0),
-    ("a", 0), ("z3", 1), ("b", 1), ("a", 1), ("s", 0), ("r1", 0), ("z4", 0), ("t", 3),
-    ("z1", 3), ("z4", 1), ("s", 1), ("r1", 1), ("r2", 0), ("t", 2), ("z1", 2), ("z2", 3),
-    ("b", 2), ("r2", 1), ("a", 2), ("b", 3), ("r3", 0), ("z2", 2), ("s", 2), ("r1", 2),
-    ("a", 3), ("r3", 1), ("z3", 3), ("s", 3), ("r1", 3), ("r4", 0), ("z5", 0), ("r2", 2),
-    ("z3", 2), ("z5", 1), ("r4", 1), ("r2", 3), ("z4", 3), ("r3", 2), ("z4", 2), ("r3", 3),
-    ("z5", 3), ("r4", 2), ("z5", 2), ("r4", 3),
+    ("o", 5), ("u", 0), ("c", 0), ("u", 1), ("o", 6), ("k", 0), ("c", 1), ("l", 0), ("t", 0),
+    ("z1", 0), ("k", 1), ("l", 1), ("t", 1), ("z1", 1), ("c", 2), ("o", 7), ("z2", 0), ("u", 2),
+    ("k", 2), ("l", 2), ("z2", 1), ("u", 3), ("c", 3), ("t", 2), ("z1", 2), ("z3", 0), ("k", 3),
+    ("l", 3), ("b", 0), ("t", 3), ("z1", 3), ("a", 0), ("s", 0), ("r1", 0), ("z2", 2), ("b", 1),
+    ("z4", 0), ("a", 1), ("b", 2), ("z2", 3), ("r2", 0), ("a", 2), ("b", 3), ("s", 2),
+    ("r1", 2), ("z3", 2), ("s", 1), ("r1", 1), ("a", 3), ("s", 3), ("r1", 3), ("r3", 0),
+    ("z5", 0), ("z3", 1), ("r2", 2), ("z3", 3), ("r2", 1), ("r2", 3), ("z4", 2), ("r4", 0),
+    ("z4", 1), ("r3", 2), ("z4", 3), ("r3", 1), ("z5", 2), ("r3", 3), ("r4", 2), ("z5", 1),
+    ("r4", 1), ("r4", 3), ("z5", 3),
 )
 
 
@@ -49,7 +49,7 @@
     rig_ref, cg_ref,
     ag, mb, core, zc, st, gs, lw, zct, bk, sel, selt, gc, asg, code, gts,
     z1, zs1, z2p, z2, z3, z4, rs1, rs2, rs3,
-    core_sem, p1_s, p1_r, ag_s, ag_r, mt_s, mt_r, d2_s, d2_r, z_s, z_r, rs_s, rs_r,
+    rigv, cgv, own_sem, out_sem, core_sem, p1_s, p1_r, ag_s, ag_r, mt_s, mt_r, d2_s, d2_r, z_s, z_r, rs_s, rs_r,
 ):
     z = lax.axis_index("dp")
     ei = lax.axis_index("expert")
@@ -88,10 +88,17 @@
         twin, to_x(1), to_x(-1), to_x(2), to_y(1), to_y(-1), to_y(2), to_z(1), to_z(-1)
     ):
         pl.semaphore_signal(barrier, inc=1, device_id=device, device_id_type=MESH)
+
+    def own_copy(n):
+        src = h_ref if n < NQ else r_ref
+        return pltpu.make_async_copy(src.at[:, cols(n % NQ)], ag.at[n, y, x], own_sem.at[n])
+
+    for n in range(NQ):
+        own_copy(n).start()
     core_copy = pltpu.make_async_copy(cores_ref, core, core_sem)
     core_copy.start()
-    for n in range(NQ):
-        ag[n, y, x] = h_ref[:, n * CQ:(n + 1) * CQ]
+    for n in range(NQ, 2 * NQ):
+        own_copy(n).start()
     mb[0, y, x] = jnp.concatenate(
         [ids_ref[...].astype(F32), gates_ref[...].astype(F32)], axis=0
     ).astype(BF16)
@@ -229,17 +236,14 @@
         lax.fori_loop(0, 2 * NS, weigh, 0)
 
     def compact(n):
-        def one(ys, carry):
-            for xs in range(NX):
-                s = ys * NX + xs
-                rows = jnp.dot(sel[s], ag[n, ys, xs], preferred_element_type=F32).astype(BF16)
-                zc[n, 0, 0, s] = rows[0:32]
-                zc[n, 0, 1, s] = rows[32:64]
-                st[n, 0, s] = rows[64:96]
-                st[n, 1, s] = rows[96:128]
-            return carry
-
-        lax.fori_loop(0, NY, one, 0)
+        for s in range(NS):
+            rows = jnp.dot(
+                sel[s], ag[n, s // NX, s % NX], preferred_element_type=F32
+            ).astype(BF16)
+            zc[n, 0, 0, s] = rows[0:32]
+            zc[n, 0, 1, s] = rows[32:64]
+            st[n, 0, s] = rows[64:96]
+            st[n, 1, s] = rows[96:128]
 
     def turn(n, rel):
         for e in (0, 1):
@@ -257,17 +261,14 @@
         when(n >= 1, other)
 
     def compute_upper(q):
-        def one(i, carry):
-            e, rel = lax.div(i, 2), lax.rem(i, 2)
-            rows = jnp.concatenate(
-                [zc[n, rel, e].reshape(ROWS, CQ) for n in range(NQ)], axis=1
-            )
-            gs[q, e, pl.ds(pl.multiple_of(rel * ROWS, ROWS), ROWS), :] = jnp.dot(
-                rows, core[e, :, cols(q)], preferred_element_type=F32
-            )
-            return carry
-
-        lax.fori_loop(0, 4, one, 0)
+        for e in (0, 1):
+            for rel in (0, 1):
+                rows = jnp.concatenate(
+                    [zc[n, rel, e].reshape(ROWS, CQ) for n in range(NQ)], axis=1
+                )
+                gs[q, e, pl.ds(rel * ROWS, ROWS), :] = jnp.dot(
+                    rows, core[e, :, cols(q)], preferred_element_type=F32
+                )
 
     def gather_r(q):
         ag_done(NQ + q)
@@ -295,13 +296,10 @@
         lax.fori_loop(0, ROWS // step, lower, 0)
 
     def form_term(q):
-        def term(i, carry):
-            e, m = lax.div(i, 2), lax.rem(i, 2)
-            at = pl.ds(pl.multiple_of(m * 512, 512), 512)
-            gs[q, e, at, :] = jnp.dot(zct[e, at, :], lw[q, e], preferred_element_type=F32)
-            return carry
-
-        lax.fori_loop(0, 4, term, 0)
+        for e in (0, 1):
+            for m in (0, 1):
+                at = pl.ds(m * 512, 512)
+                gs[q, e, at, :] = jnp.dot(zct[e, at, :], lw[q, e], preferred_element_type=F32)
 
     def z_msg(q, k, s):
         i = 0 if s > 0 else 1
@@ -311,6 +309,11 @@
         j = (k - 1) * 2 + i
         return rcopy(src.at[q, i], dst.at[q, i], z_s.at[q, j], z_r.at[q, j], to_z(s))
 
+    def out_copy(which, i):
+        if which:
+            return pltpu.make_async_copy(cgv.at[i], cg_ref.at[:, :, cols(i)], out_sem.at[1, i])
+        return pltpu.make_async_copy(rigv.at[i], rig_ref.at[:, cols(i)], out_sem.at[0, i])
+
     def part_of(d):
         return pl.ds(pl.multiple_of(d * TOK, TOK), TOK)
 
@@ -320,7 +323,8 @@
             for i, s in ((0, 1), (1, -1)):
                 z_msg(q, 4, s).wait_recv()
                 total = total + z4[q, i].astype(F32)
-            cg_ref[:, :, cols(q)] = total
+            cgv[q] = total
+            out_copy(1, q).start()
             return
         for i, s in ((0, 1), (1, -1)):
             if k == 1:
@@ -338,7 +342,7 @@
             z_msg(q, k, s).start()
 
     def form_back(b, rel):
-        def back(e, carry):
+        for e in (0, 1):
             rows = jnp.concatenate(
                 [lw[q, e, pl.ds(rel * ROWS, ROWS), :] for q in range(NQ)], axis=1
             )
@@ -351,23 +355,17 @@
                 st[b, e] = rows
             else:
                 bk[b, e] = rows
-            return carry
-
-        lax.fori_loop(0, 2, back, 0)
         if rel == 1:
             d2_back(b).start()
 
     def scatter_b(b):
         d2_back(b).wait_recv()
 
-        def scatter(ys, carry):
-            for xs in range(NX):
-                s = ys * NX + xs
-                rows = bk[b, :, s].reshape(4 * CAP, CQ)
-                ag[b, ys, xs] = jnp.dot(selt[s], rows, preferred_element_type=F32).astype(BF16)
-            return carry
-
-        lax.fori_loop(0, NY, scatter, 0)
+        for s in range(NS):
+            rows = bk[b, :, s].reshape(4 * CAP, CQ)
+            ag[b, s // NX, s % NX] = jnp.dot(
+                selt[s], rows, preferred_element_type=F32
+            ).astype(BF16)
 
     def rs_msg(b, k, half, s):
         i = 0 if s > 0 else 1
@@ -431,19 +429,22 @@
                 lax.fori_loop(0, 4, merge, 0)
                 for j in range(3):
                     last_msg(b, half, j).start()
-            else:
+            elif k == 4:
                 total = ag[b, y, x, whole].astype(F32)
                 for j in range(3):
                     last_msg(b, half, j).wait_recv()
                     total = total + rs3[b, half, j].astype(F32)
-                rig_ref[whole, cols(b)] = total.astype(BF16)
-
+                rigv[b, whole] = total.astype(BF16)
+        if k == 4:
+            out_copy(0, b).start()
+
+    own_copy(0).wait()
     near(0, "start")
     for k in range(3):
         mt_msg(k).start()
+    for n in range(1, NQ):
+        own_copy(n).wait()
     near(1, "start")
-    for n in range(NQ):
-        ag[NQ + n, y, x] = r_ref[:, n * CQ:(n + 1) * CQ]
     for k in range(3):
         mt_msg(k).wait_recv()
     for k in range(3, 6):
@@ -459,6 +460,8 @@
     core_copy.wait()
     ag_on(0)
     ag_own(2)
+    for n in range(NQ, 2 * NQ):
+        own_copy(n).wait()
     near(2, "start")
 
     def h_tick(n, carry):
@@ -529,10 +532,14 @@
         return carry
 
     lax.fori_loop(0, NQ, flushed, 0)
+    for which in (0, 1):
+        for i in range(NQ):
+            out_copy(which, i).wait()
 
 
 def local(hidden_in, rank_grad, gates, expert_ids, cores):
     vmem = pl.BlockSpec(memory_space=pltpu.VMEM)
+    hbm = pl.BlockSpec(memory_space=pl.ANY)
     dma = pltpu.SemaphoreType.DMA
     rig, cg = pl.pallas_call(
         body,
@@ -540,8 +547,8 @@
             jax.ShapeDtypeStruct((TOK, NQ * CQ), BF16),
             jax.ShapeDtypeStruct((2, TOK, NQ * CQ), F32),
         ),
-        in_specs=[vmem, vmem, vmem, vmem, pl.BlockSpec(memory_space=pl.ANY)],
-        out_specs=(vmem, vmem),
+        in_specs=[hbm, hbm, vmem, vmem, hbm],
+        out_specs=(hbm, hbm),
         scratch_shapes=[
             pltpu.VMEM((2 * NQ, NY, NX, TOK, CQ), BF16),
             pltpu.VMEM((2, NY, NX, 16, TOK), BF16),
@@ -567,6 +574,9 @@
             pltpu.VMEM((NQ, 2, 2, 4, 32, CQ), BF16),
             pltpu.VMEM((NQ, 2, 2, 4, 64, CQ), BF16),
             pltpu.VMEM((NQ, 2, 3, 64, CQ), BF16),
+            pltpu.VMEM((NQ, TOK, CQ), BF16),
+            pltpu.VMEM((NQ, 2, TOK, CQ), F32),
+            dma((2 * NQ,)), dma((2, NQ)),
             dma, dma((3, 6)), dma((3, 6)), dma((2 * NQ, 8)), dma((2 * NQ, 8)), dma((7,)), dma((7,)),
             dma((3 * NQ,)), dma((3 * NQ,)), dma((NQ, 8)), dma((NQ, 8)),
             dma((NQ, 14)), dma((NQ, 14)),

time: 112 us -> 107 us (0.955); the launches traced: 111 us -> 107 us
  Pallas kernels: 105 us -> 102 us
    pallas_call x1, Pallas kernels: 105 us -> 102 us  [local(): pl.pallas_call(body, out_shape=(jax.ShapeDtypeStruct((TOK, NQ * CQ), BF16...]
where the time goes in v4:
time: 107 us
  Pallas kernels  102 us (95%)
  local copies, waits for them, and re-layouts  4.67 us (4%)
    pallas_call x1, Pallas kernels, local(): pl.pallas_call(body, out_shape=(jax.ShapeDtypeStruct((TOK, NQ * CQ), BF16...  102 us
    unnamed x2, local copies, waits for them, and re-layouts  4.67 us

profile of v4, /device:TPU:1, one launch (start us, length us, event | category | flops | bytes accessed | tf_op | source)
XLA Modules:
  0.0 107.3 jit_solution(4139319998964888749)
XLA Ops:
  0.6 102.0 %moe_core_backward.1 = (bf16[128,1024]{1,0:T(8,128)(2,1)}, f32[2,128,1024]{2,1,0:T(8,128)}) custom-call(bf16[128,1024]{1,0:T(8,128)(2,1)} %h_ref.1, bf16[128,1024]{1,0:T(8,128)(2,1)} %r_ref.1, s32[8,128]{1,0:T(8,128)} %bitcast.4, bf16[8,128]{1,0:T(8,128)(2,1)} %bitcast.5, bf16[2,1024,1024]{2,1,0:T(8,128)(2,1)} %cores_ref.1), custom_call_target="tpu_custom_call" | custom-call | flops 14000000000 | bytes 8000000 | tf_op jit(solution)/shard_map/moe_core_backward/pallas_call | solution.py:544
  102.6 3.0 %copy.7 = f32[128,2,1024]{2,1,0:T(2,128)} copy(f32[128,2,1024]{2,0,1:T(8,128)} %bitcast.3) | data formatting | bytes 2097152
  105.6 1.7 %copy.9 = bf16[128,1024]{1,0:T(8,128)(2,1)} copy(bf16[128,1024]{1,0:T(8,128)(2,1)} %get-tuple-element.10) | data formatting | bytes 524288

commit v5 on v4

--- a/solution.py
+++ b/solution.py
@@ -108,17 +108,47 @@
     HOPS = (1, -1, 2)
     GROUPS = ((0, 1), (1, NQ - 1), (NQ, NQ))
 
+    RELAYED = 2
+
     def near_msg(g, half, j):
         lo, count = GROUPS[g]
-        ref = ag.at[pl.ds(lo, count), y, x, pl.ds(half * 64, 64)]
-        k = half * 3 + j
-        device = to_x(HOPS[j]) if half == 0 else to_y(HOPS[j])
+        rounds = pl.ds(lo, count)
+        o = half * 64
+        if g < RELAYED:
+            hop = HOPS[j]
+            ref = ag.at[rounds, y, x, pl.ds(o, 64)]
+        else:
+            hop = HOPS[j % 2]
+            if j < 2:
+                ref = ag.at[rounds, y, x, pl.ds(o, 64)]
+            else:
+                part = pl.ds(o + 32 * (j - 2), 32)
+                yy, xx = (y, wx(x - hop)) if half == 0 else (wx(y - hop), x)
+                ref = ag.at[rounds, yy, xx, part]
+        k = half * 4 + j
+        device = to_x(hop) if half == 0 else to_y(hop)
         return rcopy(ref, ref, p1_s.at[g, k], p1_r.at[g, k], device)
 
     def near(g, act):
+        count = 3 if g < RELAYED else 4 if act == "wait_send" else 2
         for half in (0, 1):
-            for j in range(3):
+            for j in range(count):
                 getattr(near_msg(g, half, j), act)()
+
+    def near_on(g):
+        if g >= RELAYED:
+            for half in (0, 1):
+                for j in (0, 1):
+                    near_msg(g, half, j).wait_recv()
+                    near_msg(g, half, j + 2).start()
+
+    def near_done(g):
+        if g < RELAYED:
+            near(g, "wait_recv")
+        else:
+            for half in (0, 1):
+                for j in (2, 3):
+                    near_msg(g, half, j).wait_recv()
 
     def ag_msg(n, kind, half, s):
         o = half * 64
@@ -451,7 +481,7 @@
         mt_msg(k).start()
     near(0, "wait_recv")
     ag_own(0)
-    near(1, "wait_recv")
+    near_done(1)
     ag_own(1)
     for k in range(3, 6):
         mt_msg(k).wait_recv()
@@ -466,8 +496,9 @@
 
     def h_tick(n, carry):
         ag_on(n)
-        when(n == 2, lambda: near(2, "wait_recv"))
+        when(n == 2, lambda: near_done(2))
         ag_own(n + 2)
+        when(n == 1, lambda: near_on(2))
         ag_done(n - 1)
         compute_h(n - 1)
         return carry
@@ -535,6 +566,12 @@
     for which in (0, 1):
         for i in range(NQ):
             out_copy(which, i).wait()
+
+
+def finish(rig_ref, cg_ref, rig_out, cg_out):
+    rig_out[...] = rig_ref[...]
+    for e in (0, 1):
+        cg_out[:, e, :] = cg_ref[e]
 
 
 def local(hidden_in, rank_grad, gates, expert_ids, cores):
@@ -577,7 +614,7 @@
             pltpu.VMEM((NQ, TOK, CQ), BF16),
             pltpu.VMEM((NQ, 2, TOK, CQ), F32),
             dma((2 * NQ,)), dma((2, NQ)),
-            dma, dma((3, 6)), dma((3, 6)), dma((2 * NQ, 8)), dma((2 * NQ, 8)), dma((7,)), dma((7,)),
+            dma, dma((3, 8)), dma((3, 8)), dma((2 * NQ, 8)), dma((2 * NQ, 8)), dma((7,)), dma((7,)),
             dma((3 * NQ,)), dma((3 * NQ,)), dma((NQ, 8)), dma((NQ, 8)),
             dma((NQ, 14)), dma((NQ, 14)),
         ],
@@ -589,7 +626,25 @@
         ),
         name="moe_core_backward",
     )(hidden_in, rank_grad, expert_ids.T, gates.T, cores)
-    return rig, jnp.transpose(cg, (1, 0, 2))
+    part = TOK // 1
+    return pl.pallas_call(
+        finish,
+        grid=(1,),
+        out_shape=(
+            jax.ShapeDtypeStruct((TOK, NQ * CQ), BF16),
+            jax.ShapeDtypeStruct((TOK, 2, NQ * CQ), F32),
+        ),
+        in_specs=[
+            pl.BlockSpec((part, NQ * CQ), lambda i: (i, 0)),
+            pl.BlockSpec((2, part, NQ * CQ), lambda i: (0, i, 0)),
+        ],
+        out_specs=(
+            pl.BlockSpec((part, NQ * CQ), lambda i: (i, 0)),
+            pl.BlockSpec((part, 2, NQ * CQ), lambda i: (i, 0, 0)),
+        ),
+        compiler_params=pltpu.CompilerParams(vmem_limit_bytes=16 * 1024 * 1024),
+        name="place_outputs",
+    )(rig, cg)
 
 
 def solution(mesh):

time: 107 us -> 106 us (level)
  local copies, waits for them, and re-layouts: 4.67 us -> 2.17 us
    unnamed x2 -> x4, local copies, waits for them, and re-layouts: 4.67 us -> 2.17 us
    pallas_call x0 -> x1, Pallas kernels: none -> 1.16 us  [local(): pl.pallas_call(finish, grid=(1,), out_shape=(jax.ShapeDtypeStruct((TOK, N...]
where the time goes in v5:
time: 106 us; the launch traced here: 105 us
  Pallas kernels  103 us (97%)
  local copies, waits for them, and re-layouts  2.17 us (2%)
    pallas_call x1, Pallas kernels, local(): pl.pallas_call(body, out_shape=(jax.ShapeDtypeStruct((TOK, NQ * CQ), BF16...  101 us
    unnamed x4, local copies, waits for them, and re-layouts  2.17 us

profile of v5, /device:TPU:1, one launch (start us, length us, event | category | flops | bytes accessed | tf_op | source)
XLA Modules:
  0.0 105.3 jit_solution(10635796094340921924)
XLA Ops:
  0.6 101.4 %moe_core_backward.1 = (bf16[128,1024]{1,0:T(8,128)(2,1)}, f32[2,128,1024]{2,1,0:T(8,128)}) custom-call(bf16[128,1024]{1,0:T(8,128)(2,1)} %h_ref.1, bf16[128,1024]{1,0:T(8,128)(2,1)} %r_ref.1, s32[8,128]{1,0:T(8,128)} %bitcast.2, bf16[8,128]{1,0:T(8,128)(2,1)} %bitcast.3, bf16[2,1024,1024]{2,1,0:T(8,128)(2,1)} %cores_ref.1), custom_call_target="tpu_custom_call" | custom-call | flops 14000000000 | bytes 8000000 | tf_op jit(solution)/shard_map/moe_core_backward/pallas_call | solution.py:581
  102.0 0.0 copy-start
  102.0 1.2 %copy-done = f32[2,128,1024]{2,1,0:T(8,128)S(1)} copy-done((f32[2,128,1024]{2,1,0:T(8,128)S(1)}, f32[2,128,1024]{2,1,0:T(8,128)}, u32[]{:S(2)}) %copy-start) | copy-done | bytes 1048600
  103.2 0.0 copy-start.1
  103.2 0.9 copy-done.1
  104.2 1.2 %place_outputs.1 = (bf16[128,1024]{1,0:T(8,128)(2,1)}, f32[128,2,1024]{2,1,0:T(2,128)}) custom-call(bf16[128,1024]{1,0:T(8,128)(2,1)S(1)} %copy-done.1, f32[2,128,1024]{2,1,0:T(8,128)S(1)} %copy-done), custom_call_target="tpu_custom_call" | custom-call | tf_op jit(solution)/shard_map/place_outputs/pallas_call | solution.py:630
Async XLA Ops:
  102.0 1.2 %copy-start = (f32[2,128,1024]{2,1,0:T(8,128)S(1)}, f32[2,128,1024]{2,1,0:T(8,128)}, u32[]{:S(2)}) copy-start(f32[2,128,1024]{2,1,0:T(8,128)} %get-tuple-element.5.cg_ref) | copy-start | bytes 3145732
  103.2 0.9 copy-start.1
